TPU v7x, 512 devices: a whole 4x8x8 slice. The times are simulated.
512 devices in a mesh: pb: 8 (over y), ka: 16 (over z, core), ha: 4 (over x).
Axes of the slice: x: 4, y: 8, z: 8, core: 2. Of those that a mesh axis runs over, the one named last changes fastest.
Arguments:
- latent: bfloat16 [2048, 1536], P('pb'), may hold values from -6 to 6
- query_weight: bfloat16 [1536, 8192], P(None, ('ka', 'ha')), may hold values from -0.15625 to 0.15625
- head_weights: bfloat16 [2048, 64], P('pb', ('ka', 'ha')), may hold values from -0.75 to 0.75
- raw_keys: bfloat16 [65536, 128], P(('ka', 'ha')), may hold values from -6 to 6
- key_gain: float32 [128], replicated, may hold values from 0.1 to 1.9
- key_bias: float32 [128], replicated, may hold values from -3 to 3
- query_start: int32 [8], P('pb'), may hold values from 0 to 65280, as said below
- key_order: int32 [16], P('ka'), may hold values from 0 to 15, each once
Outputs:
- index_scores: float32 [2048, 65536], P('pb', ('ka', 'ha'))
Inputs may be any that keep to these rules, and one draw needn't show every extreme that they name: `query_start`: entries are distinct multiples of 256; the last block (position 65280) is always among them. `key_order`: each block number 0 to 15 appears exactly once.
All inputs are finite; a program needn't handle non-finite values.
Results may differ from a plain program's by a relative error of at most 0.007.
Values may be sent and summed in bfloat16 or wider, within the bound.
No kernel may reach another device: no remote copies, remote signals or barrier semaphores. Data moves between devices by JAX's collectives and lax.ppermute only.
A program may use at most 128 MiB of HBM per device.

v0:
```python
import jax
import jax.numpy as jnp
from jax import lax
from jax.sharding import PartitionSpec as P


def normalize_keys(raw_keys, key_gain, key_bias):
    values = raw_keys.astype(jnp.float32)
    center = jnp.mean(values, axis=-1, keepdims=True)
    spread = jnp.mean(jnp.square(values - center), axis=-1, keepdims=True)
    scaled = (values - center) * lax.rsqrt(spread + 1e-06)
    return (scaled * key_gain + key_bias).astype(jnp.bfloat16)


def score_tile(queries, weights, tile_keys, query_pos, key_pos):
    total_rows = queries.shape[0]
    head_dim = tile_keys.shape[1]
    head_count = queries.shape[1] // head_dim
    grouped = queries.reshape(total_rows, head_count, head_dim)
    weights_full = weights.astype(jnp.float32)
    key_count = tile_keys.shape[0]
    block_width = 512
    blocks = key_count // block_width

    def one_block(block_pair):
        part_keys, part_pos = block_pair
        scores = jnp.einsum("qhd,kd->qhk", grouped, part_keys, preferred_element_type=jnp.float32)
        active = jax.nn.relu(scores) * head_dim ** (-0.5)
        totals = jnp.einsum("qhk,qh->qk", active, weights_full)
        return jnp.where(part_pos[None, :] <= query_pos[:, None], totals, jnp.zeros_like(totals))

    tiles = lax.map(
        one_block,
        (tile_keys.reshape(blocks, block_width, head_dim), key_pos.reshape(blocks, block_width)),
    )
    return tiles.transpose(1, 0, 2).reshape(total_rows, key_count)


def per_device(
    latent, query_weight, head_weights, raw_keys, key_gain, key_bias, query_start, key_order
):
    local_queries = jnp.dot(latent, query_weight, preferred_element_type=jnp.float32).astype(
        jnp.bfloat16
    )
    normed = normalize_keys(raw_keys, key_gain, key_bias)
    query_rows = latent.shape[0]
    local_keys = raw_keys.shape[0]
    block_span = local_keys * lax.axis_size("ha")
    query_pos = query_start[0] + jnp.arange(query_rows, dtype=jnp.int32)
    block_begin = key_order[0] * block_span
    all_queries, all_weights = (
        lax.all_gather(local_queries, ("ka", "ha"), axis=1, tiled=True),
        lax.all_gather(head_weights, ("ka", "ha"), axis=1, tiled=True),
    )
    key_pos = (
        block_begin + lax.axis_index("ha") * local_keys + jnp.arange(local_keys, dtype=jnp.int32)
    )
    result = score_tile(all_queries, all_weights, normed, query_pos, key_pos)
    return result


def solution(mesh):
    in_specs = (
        P("pb", None),
        P(None, ("ka", "ha")),
        P("pb", ("ka", "ha")),
        P(("ka", "ha"), None),
        P(),
        P(),
        P("pb"),
        P("ka"),
    )
    out_specs = P("pb", ("ka", "ha"))
    return jax.shard_map(
        per_device, mesh=mesh, in_specs=in_specs, out_specs=out_specs, check_vma=False
    )
```

profile of v0, /device:TPU:1, one launch (start us, length us, event | category | flops | bytes accessed | tf_op | source)
XLA Modules:
  0.0 195.5 jit_solution(8388475526039756181)
XLA Ops:
  6.5 0.0 copy-start
  6.5 0.0 all-gather.3.cloned.1.call-start
  6.5 1.1 copy-done
  7.7 2.0 %convolution_convert_fusion = bf16[256,128]{1,0:T(8,128)(2,1)} fusion(bf16[256,1536]{1,0:T(8,128)(2,1)S(1)} %copy-done, bf16[1536,128]{1,0:T(8,128)(2,1)} %param.11), kind=kOutput, calls=%fused_computation.10 | convolution fusion | flops 100696064 | bytes 1245184 | tf_op jit(solution)/shard_map/dot_general | solution.py:42
  9.6 0.0 all-gather.3.cloned.1.call-update
  9.7 81.4 %all-gather = bf16[64,1,256]{2,1,0:T(2,128)(2,1)S(1)} all-gather(bf16[1,1,256]{2,1,0:T(2,128)(2,1)} %bitcast.60), channel_id=1, replica_groups=mesh['pb'=8,'ka'=16,'ha'=4] {'ka','ha'}, dimensions={0}, use_global_device_ids=true | all-gather | bytes 33280 | tf_op jit(solution)/shard_map/all_gather | solution.py:53
  91.1 0.1 copy.19
  91.9 1.1 convert_reduce_fusion
  93.0 1.3 fusion.7
  94.3 1.3 fusion.10
  95.6 3.7 %all-gather.3.cloned.1.call-done = bf16[256,8192]{1,0:T(8,128)(2,1)} async-done(((bf16[256,128]{1,0:T(8,128)(2,1)}), bf16[256,8192]{1,0:T(8,128)(2,1)}) %all-gather.3.cloned.1.call-update) | async-done | bytes 4194320 | tf_op jit(solution)/shard_map/all_gather | solution.py:52
  99.3 5.4 %copy_bitcast_fusion = bf16[256,64,128]{2,0,1:T(8,128)(2,1)} fusion(bf16[256,8192]{1,0:T(8,128)(2,1)} %all-gather.3.cloned.1.call-done), kind=kLoop, calls=%fused_computation.9 | loop fusion | bytes 8388608
  104.8 82.9 %while.11 = (s32[]{:T(128)}, f32[2,256,512]{2,1,0:T(8,128)S(1)}, s32[2,512]{1,0:T(2,128)S(1)}, bf16[2,512,128]{2,1,0:T(8,128)(2,1)S(1)}, bf16[256,64,128]{2,0,1:...) while((s32[]{:T(128)}, f32[2,256,512]{2,1,0:T(8,128)S(1)}, ...), condition=%wide.region_3.4_spmd.clone, body=%wide.region_2.3_spmd.clone.sunk | while | flops 2189689088 | bytes 73080920 | solution.py:32
  104.8 10.2 %multiply_bitcast_fusion.2 = bf16[256,64,512]{0,2,1:T(8,128)(2,1)} fusion(bf16[256,64,128]{2,0,1:T(8,128)(2,1)} %get-tuple-element.151, bf16[2,512,128]{2,1,0:T(8,128)(2,1)S(1)} %get-tuple-element.150, s32[]{:T(128)} %get-tuple-element.139), kind=kOutput, calls=%fused_computation.1.clone.1 | convolution fusion | flops 2172649472 | bytes 21102596 | tf_op jit(solution)/shard_map/while/body/eval_jaxpr/qhd,kd->qhk/dot_general | solution.py:27
  115.0 23.4 %copy.27 = bf16[256,64,512]{2,1,0:T(8,128)(2,1)} copy(bf16[256,64,512]{0,2,1:T(8,128)(2,1)} %multiply_bitcast_fusion.2) | data formatting | bytes 33554432 | tf_op jit(solution)/shard_map/while/body/eval_jaxpr/mul | solution.py:28
  138.4 7.0 %fusion.27 = f32[256,1,512]{2,1,0:T(1,128)S(1)} fusion(bf16[256,64,512]{2,1,0:T(8,128)(2,1)} %copy.27, f32[256,64,1]{1,2,0:T(1,128)S(1)} %bitcast.56), kind=kOutput, calls=%fused_computation.22.clone.1 | convolution fusion | flops 16777216 | bytes 17367040 | tf_op jit(solution)/shard_map/while/body/eval_jaxpr/qhk,qh->qk/dot_general | solution.py:29
  145.4 0.7 iota_add_fusion.2
  146.1 0.1 bitcast_dynamic-update-slice_fusion.2
  146.2 10.3 %multiply_bitcast_fusion.2 = bf16[256,64,512]{0,2,1:T(8,128)(2,1)} fusion(bf16[256,64,128]{2,0,1:T(8,128)(2,1)} %get-tuple-element.151, bf16[2,512,128]{2,1,0:T(8,128)(2,1)S(1)} %get-tuple-element.150, s32[]{:T(128)} %get-tuple-element.139), kind=kOutput, calls=%fused_computation.1.clone.1 | convolution fusion | flops 2172649472 | bytes 21102596 | tf_op jit(solution)/shard_map/while/body/eval_jaxpr/qhd,kd->qhk/dot_general | solution.py:27
  156.4 23.4 %copy.27 = bf16[256,64,512]{2,1,0:T(8,128)(2,1)} copy(bf16[256,64,512]{0,2,1:T(8,128)(2,1)} %multiply_bitcast_fusion.2) | data formatting | bytes 33554432 | tf_op jit(solution)/shard_map/while/body/eval_jaxpr/mul | solution.py:28
  179.9 7.0 %fusion.27 = f32[256,1,512]{2,1,0:T(1,128)S(1)} fusion(bf16[256,64,512]{2,1,0:T(8,128)(2,1)} %copy.27, f32[256,64,1]{1,2,0:T(1,128)S(1)} %bitcast.56), kind=kOutput, calls=%fused_computation.22.clone.1 | convolution fusion | flops 16777216 | bytes 17367040 | tf_op jit(solution)/shard_map/while/body/eval_jaxpr/qhk,qh->qk/dot_general | solution.py:29
  186.9 0.7 iota_add_fusion.2
  187.5 0.1 bitcast_dynamic-update-slice_fusion.2
  187.6 1.1 copy.21
  (6 shorter events, 0.0 us)
Async XLA Ops:
  6.5 1.1 copy-start
  6.5 92.8 %all-gather.3.cloned.1.call-start = ((), (), s32[]{:S(2)}) async-start(), calls=%async_computation | async-start | bytes 4259840 | tf_op jit(solution)/shard_map/all_gather | solution.py:52
Sparse Core Ops, SparseCore 0:
  10.5 88.7 all-gather.2
where the time goes:
time: 197 us; the launch traced here: 196 us
  blocking collectives  81.4 us (41%)
  local copies, waits for them, and re-layouts  54.6 us (28%)
  matrix products  36.4 us (18%)
  between operations  14.1 us (7%)
  other arithmetic  5.25 us (3%)
  waiting for transfers between devices  3.75 us (2%)
    all_gather x1, blocking collectives, per_device(): lax.all_gather(head_weights, ('ka', 'ha'), axis=1, tiled=True)  81.4 us
    mul x2, local copies, waits for them, and re-layouts, one_block(): active = jax.nn.relu(scores) * head_dim ** (-0.5)  46.8 us
    dot_general x2, matrix products, one_block(): jnp.einsum('qhd,kd->qhk', grouped, part_keys, preferred_element_type=jnp....  20.5 us
    dot_general x2, matrix products, one_block(): totals = jnp.einsum('qhk,qh->qk', active, weights_full)  13.9 us
    unnamed x3, local copies, waits for them, and re-layouts  6.55 us
  transfers between devices with their start and end apart: 1, of which 1 were waited for; matrix products, arithmetic and copies ran while one was open for 2% of the time, Pallas kernels for 0%

commit v1 on v0

v1 whole, which is shorter than its diff:
```python
import functools

import jax
import jax.numpy as jnp
from jax import lax
from jax.experimental import pallas as pl
from jax.experimental.pallas import tpu as pltpu
from jax.sharding import PartitionSpec as P

VMEM = pltpu.VMEM
SMEM = pltpu.SMEM
TOKENS = 256
KEYS = 1024
HDIM = 128
ROWS = TOKENS + 16
TB = 32
AHEAD = 6
FLAT = ("ka", "ha")


def front_kernel(latent_ref, weight_ref, head_ref, raw_ref, gain_ref, bias_ref, block_ref, keys_ref):
    queries = jnp.dot(
        latent_ref[...], weight_ref[...], preferred_element_type=jnp.float32
    ).astype(jnp.bfloat16)
    row = head_ref[...].astype(jnp.float32)
    row_at = lax.broadcasted_iota(jnp.int32, (16, HDIM), 0)
    first = jnp.broadcast_to(row[:, :HDIM], (16, HDIM))
    second = jnp.broadcast_to(row[:, HDIM:], (16, HDIM))
    tail = jnp.where(row_at == 0, first, jnp.where(row_at == 1, second, 0.0)).astype(jnp.bfloat16)
    for i in range(block_ref.shape[0]):
        block_ref[i, :TOKENS, :] = queries
        block_ref[i, TOKENS:, :] = tail
    values = raw_ref[...].astype(jnp.float32)
    center = jnp.mean(values, axis=-1, keepdims=True)
    moved = values - center
    spread = jnp.mean(jnp.square(moved), axis=-1, keepdims=True)
    scaled = moved * lax.rsqrt(spread + 1e-06)
    keys_ref[...] = (scaled * gain_ref[...] + bias_ref[...]).astype(jnp.bfloat16)


def front(latent, query_weight, head_row, raw_keys, gain, bias, copies):
    return pl.pallas_call(
        front_kernel,
        out_shape=(
            jax.ShapeDtypeStruct((copies, ROWS, HDIM), jnp.bfloat16),
            jax.ShapeDtypeStruct((KEYS, HDIM), jnp.bfloat16),
        ),
        in_specs=[pl.BlockSpec(memory_space=VMEM)] * 6,
        out_specs=[pl.BlockSpec(memory_space=VMEM)] * 2,
        compiler_params=pltpu.CompilerParams(vmem_limit_bytes=24 * 2**20),
        cost_estimate=pl.CostEstimate(flops=2 * 256 * 1536 * 128, bytes_accessed=2 * 2**20, transcendentals=1024),
        name="front",
    )(latent, query_weight, head_row, raw_keys, gain, bias)


def score_kernel(*refs, chunks, has_total):
    parts = refs[:chunks]
    keys_ref = refs[chunks]
    total_ref = refs[chunks + 1] if has_total else None
    out_ref = refs[-1]
    heads = [(p, h) for p in parts for h in range(p.shape[0])]
    steps = [(t, i) for t in range(TOKENS // TB) for i in range(len(heads))]
    slots = AHEAD + 1

    def scoped(*accs):
        def acc(m, s, j):
            return accs[(m * slots + s) * 2 + j]

        for m in range(2):
            a = keys_ref[512 * m : 512 * m + 256, :]
            b = keys_ref[512 * m + 256 : 512 * m + 512, :]
            pltpu.matmul_push_rhs(jnp.concatenate([a, b], axis=1), 0, m, transpose=True)
        zero = jnp.zeros((TB, HDIM), jnp.bfloat16)
        columns = [p[h, TOKENS:, :].astype(jnp.float32).T for p, h in heads]

        def issue(n):
            t, i = steps[n]
            p, h = heads[i]
            q = p[h, t * TB : (t + 1) * TB, :]
            low = jnp.concatenate([q, zero], axis=1)
            high = jnp.concatenate([zero, q], axis=1)
            for m in range(2):
                pltpu.matmul_acc_lhs(acc(m, n % slots, 0), low, load_staged_rhs=0 if n == 0 else None)
                pltpu.matmul_acc_lhs(acc(m, n % slots, 1), high)

        for n in range(min(AHEAD, len(steps))):
            issue(n)
        sums = None
        per_row = HDIM // TB
        for n, (t, i) in enumerate(steps):
            if n + AHEAD < len(steps):
                issue(n + AHEAD)
            if i == 0:
                if total_ref is None:
                    sums = [jnp.zeros((TB, 256), jnp.float32) for _ in range(4)]
                else:
                    sums = [total_ref[t * TB : (t + 1) * TB, 256 * g : 256 * (g + 1)] for g in range(4)]
            at = (t % per_row) * TB
            weight = columns[i][at : at + TB, t // per_row : t // per_row + 1]
            weight = jnp.broadcast_to(weight, (TB, 256))
            for m in range(2):
                for j in range(2):
                    score = pltpu.matmul_pop(acc(m, n % slots, j))
                    sums[2 * m + j] = sums[2 * m + j] + jnp.maximum(score, 0.0) * weight
            if i == len(heads) - 1:
                for g in range(4):
                    out_ref[t * TB : (t + 1) * TB, 256 * g : 256 * (g + 1)] = sums[g].astype(out_ref.dtype)

    pl.run_scoped(scoped, *[pltpu.ACC(m)((TB, 256), jnp.float32) for m in range(2) for _ in range(2 * slots)])


def scores(parts, keys, total=None, out_dtype=jnp.float32, name="scores"):
    heads = sum(p.shape[0] for p in parts)
    extra = [] if total is None else [total]
    return pl.pallas_call(
        functools.partial(score_kernel, chunks=len(parts), has_total=total is not None),
        out_shape=jax.ShapeDtypeStruct((TOKENS, KEYS), out_dtype),
        in_specs=[pl.BlockSpec(memory_space=VMEM)] * (len(parts) + 1 + len(extra)),
        out_specs=pl.BlockSpec(memory_space=VMEM),
        compiler_params=pltpu.CompilerParams(vmem_limit_bytes=24 * 2**20),
        cost_estimate=pl.CostEstimate(
            flops=4 * heads * TOKENS * KEYS * HDIM, bytes_accessed=2**21, transcendentals=0
        ),
        name=name,
    )(*parts, keys, *extra)


def finish_kernel(place_ref, own_ref, other_ref, out_ref):
    scale = HDIM ** (-0.5)
    rows = out_ref.shape[0]
    query = place_ref[0] + lax.broadcasted_iota(jnp.int32, (rows, 256), 0)
    for g in range(KEYS // 256):
        key = place_ref[1] + 256 * g + lax.broadcasted_iota(jnp.int32, (rows, 256), 1)
        at = slice(256 * g, 256 * (g + 1))
        total = (own_ref[:, at] + other_ref[:, at].astype(jnp.float32)) * scale
        out_ref[:, at] = jnp.where(key <= query, total, 0.0)


def finish(place, own, other):
    return pl.pallas_call(
        finish_kernel,
        out_shape=jax.ShapeDtypeStruct((TOKENS, KEYS), jnp.float32),
        in_specs=[pl.BlockSpec(memory_space=SMEM)] + [pl.BlockSpec(memory_space=VMEM)] * 2,
        out_specs=pl.BlockSpec(memory_space=VMEM),
        compiler_params=pltpu.CompilerParams(vmem_limit_bytes=24 * 2**20),
        cost_estimate=pl.CostEstimate(flops=2**20, bytes_accessed=3 * 2**20, transcendentals=0),
        name="finish",
    )(place, own, other)


def layout(z_size, x_size):
    def flat(z, core, x):
        return ((z % z_size) * 2 + core) * x_size + x % x_size

    sites = [(z, x) for z in range(z_size) for x in range(x_size)]
    groups = [
        [flat(z, core, x) for z, x in sites if (z - x) % x_size == coset]
        for core in range(2)
        for coset in range(x_size)
    ]

    def moved(dz, dx):
        return [
            (flat(z, core, x), flat(z + sign * dz, core, x + sign * dx))
            for core, sign in ((0, 1), (1, -1))
            for z, x in sites
        ]

    swap = [(flat(z, core, x), flat(z, 1 - core, x)) for z, x in sites for core in range(2)]
    return groups, moved, swap


def per_device(
    latent, query_weight, head_weights, raw_keys, key_gain, key_bias, query_start, key_order
):
    ka, ha = lax.axis_size("ka"), lax.axis_size("ha")
    groups, moved, swap = layout(ka // 2, ha)
    block, keys = front(
        latent,
        query_weight,
        head_weights.reshape(1, TOKENS),
        raw_keys,
        key_gain.reshape(1, HDIM),
        key_bias.reshape(1, HDIM),
        len(groups[0]),
    )
    here = lax.all_to_all(block, FLAT, 0, 0, axis_index_groups=groups)
    other_keys = lax.ppermute(keys, FLAT, swap)
    along_z = lax.ppermute(here, FLAT, moved(1, 0))
    along_x = lax.ppermute(here, FLAT, moved(0, 1))
    diagonal = lax.ppermute(here, FLAT, moved(1, -1))

    own = scores([here], keys, name="own0")
    other = scores([here], other_keys, name="other0")
    other = scores([along_z], other_keys, other, name="other1")
    own = scores([along_z], keys, own, name="own1")
    other = scores([along_x], other_keys, other, name="other2")
    own = scores([along_x], keys, own, name="own2")
    other = scores([diagonal], other_keys, other, jnp.bfloat16, name="other3")
    received = lax.ppermute(other, FLAT, swap)
    own = scores([diagonal], keys, own, name="own3")
    key_begin = (key_order[0] * ha + lax.axis_index("ha")) * KEYS
    place = jnp.stack([query_start[0], key_begin]).astype(jnp.int32)
    return finish(place, own, received)


def solution(mesh):
    in_specs = (
        P("pb", None),
        P(None, ("ka", "ha")),
        P("pb", ("ka", "ha")),
        P(("ka", "ha"), None),
        P(),
        P(),
        P("pb"),
        P("ka"),
    )
    out_specs = P("pb", ("ka", "ha"))
    return jax.shard_map(
        per_device, mesh=mesh, in_specs=in_specs, out_specs=out_specs, check_vma=False
    )
```

time: 197 us -> 71.5 us (0.36)
  local copies, waits for them, and re-layouts: 54.6 us -> 3.77 us
  blocking collectives: 81.4 us -> 31.3 us
  matrix products: 36.4 us -> 0 us
  starting transfers between devices: 0.01 us -> 16.6 us
  Pallas kernels: 0 us -> 12.7 us
  between operations: 14.1 us -> 1.45 us
  other arithmetic: 5.25 us -> 0.08 us
    all_gather x1 -> x0, blocking collectives: 81.4 us -> none  [per_device(): lax.all_gather(head_weights, ('ka', 'ha'), axis=1, tiled=True)]
    mul x2 -> x0, local copies, waits for them, and re-layouts: 46.8 us -> none  [one_block(): active = jax.nn.relu(scores) * head_dim ** (-0.5)]
    dot_general x5 -> x0, matrix products: 36.4 us -> none  [the longest x2 20.5 us: one_block(): jnp.einsum('qhd,kd->qhk', grouped, part_keys, preferred_element_type=jnp....]
    all_to_all x0 -> x1, blocking collectives: none -> 31.3 us  [per_device(): here = lax.all_to_all(block, FLAT, 0, 0, axis_index_groups=groups)]
    ppermute x0 -> x5, starting transfers between devices: none -> 16.6 us  [the longest x1 4.41 us: per_device(): received = lax.ppermute(other, FLAT, swap)]
    pallas_call x0 -> x10, Pallas kernels: none -> 12.7 us  [the longest x8 10.6 us: scores(): pl.pallas_call(functools.partial(score_kernel, chunks=len(parts), has_tot...]
    ppermute x0 -> x5, waiting for transfers between devices: none -> 5.28 us  [the longest x1 5.27 us: per_device(): diagonal = lax.ppermute(here, FLAT, moved(1, -1))]
    all_gather x1 -> x0, waiting for transfers between devices: 3.73 us -> none  [per_device(): lax.all_gather(local_queries, ('ka', 'ha'), axis=1, tiled=True)]
  transfers between devices with their start and end apart: 1 -> 5, of which waited for: 1 -> 1; matrix products, arithmetic and copies ran while one was open for 2% -> 0% of each run, Pallas kernels for 0% -> 13%
where the time goes in v1:
time: 71.5 us; the launch traced here: 71.1 us
  blocking collectives  31.3 us (44%)
  starting transfers between devices  16.6 us (23%)
  Pallas kernels  12.7 us (18%)
  waiting for transfers between devices  5.28 us (7%)
  local copies, waits for them, and re-layouts  3.77 us (5%)
  between operations  1.45 us (2%)
    all_to_all x1, blocking collectives, per_device(): here = lax.all_to_all(block, FLAT, 0, 0, axis_index_groups=groups)  31.3 us
    pallas_call x8, Pallas kernels, scores(): pl.pallas_call(functools.partial(score_kernel, chunks=len(parts), has_tot...  10.6 us
    ppermute x1, waiting for transfers between devices, per_device(): diagonal = lax.ppermute(here, FLAT, moved(1, -1))  5.27 us
    ppermute x1, starting transfers between devices, per_device(): received = lax.ppermute(other, FLAT, swap)  4.41 us
    unnamed x12, local copies, waits for them, and re-layouts  3.77 us
    ppermute x1, starting transfers between devices, per_device(): other_keys = lax.ppermute(keys, FLAT, swap)  3.6 us
    ppermute x1, starting transfers between devices, per_device(): diagonal = lax.ppermute(here, FLAT, moved(1, -1))  3.4 us
    ppermute x1, starting transfers between devices, per_device(): along_x = lax.ppermute(here, FLAT, moved(0, 1))  3.16 us
  transfers between devices with their start and end apart: 5, of which 1 were waited for; matrix products, arithmetic and copies ran while one was open for 0% of the time, Pallas kernels for 13%

profile of v1, /device:TPU:1, one launch (start us, length us, event | category | flops | bytes accessed | tf_op | source)
XLA Modules:
  0.0 71.1 jit_solution(15250975013460870511)
XLA Ops:
  0.0 0.0 copy-start.5
  0.0 0.0 copy-start.3
  0.0 0.0 copy-start.4
  0.0 0.6 copy-done.5
  0.7 0.0 copy-done.3
  0.7 0.0 copy-done.4
  0.7 0.0 copy-start
  0.7 1.1 %copy-done = bf16[256,1536]{1,0:T(8,128)(2,1)S(1)} copy-done((bf16[256,1536]{1,0:T(8,128)(2,1)S(1)}, bf16[256,1536]{1,0:T(8,128)(2,1)}, u32[]{:S(2)}) %copy-start) | copy-done | bytes 786456
  1.8 0.0 copy-start.1
  1.8 1.0 %copy-done.1 = bf16[1536,128]{1,0:T(8,128)(2,1)S(1)} copy-done((bf16[1536,128]{1,0:T(8,128)(2,1)S(1)}, bf16[1536,128]{1,0:T(8,128)(2,1)}, u32[]{:S(2)}) %copy-start.1) | copy-done | bytes 393240
  2.8 0.0 copy-start.2
  2.8 0.9 %copy-done.2 = bf16[1024,128]{1,0:T(8,128)(2,1)S(1)} copy-done((bf16[1024,128]{1,0:T(8,128)(2,1)S(1)}, bf16[1024,128]{1,0:T(8,128)(2,1)}, u32[]{:S(2)}) %copy-start.2) | copy-done | bytes 262168
  3.8 0.4 front.1
  4.2 31.3 %all_to_all.5.refs_0_ = bf16[8,272,128]{2,1,0:T(8,128)(2,1)S(1)} all-to-all(bf16[8,272,128]{2,1,0:T(8,128)(2,1)S(1)} %get-tuple-element.7), channel_id=1, replica_groups={{0,9,18,27,32,41,50,59},{3,8,17,26,35,40,49,58},{2,11,16,25,34,43,48,57..., dimensions={0} | all-to-all | bytes 1114112 | tf_op jit(solution)/shard_map/all_to_all | solution.py:187
  35.5 2.0 %collective-permute-start.2 = (bf16[8,272,128]{2,1,0:T(8,128)(2,1)S(1)}, bf16[8,272,128]{2,1,0:T(8,128)(2,1)S(1)}, u32[]{:S(2)}, u32[]{:S(2)}) collective-permute-start(bf16[8,272,128]{2,1,0:T(8,128)(2,1)S(1)} %all_to_all.5.refs_0_), channel_id=1, source_target_pairs={{0,8},{1,9},{2,10},{3,11},{8,16},{9,17},{10,18},{11,19},{16,24},{1... | collective-permute-start | bytes 1671176 | tf_op jit(solution)/shard_map/ppermute | solution.py:189
  37.4 3.2 %collective-permute-start.1 = (bf16[8,272,128]{2,1,0:T(8,128)(2,1)S(1)}, bf16[8,272,128]{2,1,0:T(8,128)(2,1)S(1)}, u32[]{:S(2)}, u32[]{:S(2)}) collective-permute-start(bf16[8,272,128]{2,1,0:T(8,128)(2,1)S(1)} %all_to_all.5.refs_0_), channel_id=1, source_target_pairs={{0,1},{1,2},{2,3},{3,0},{8,9},{9,10},{10,11},{11,8},{16,17},{17,18... | collective-permute-start | bytes 1671176 | tf_op jit(solution)/shard_map/ppermute | solution.py:190
  40.6 3.6 %collective-permute-start.3 = (bf16[1024,128]{1,0:T(8,128)(2,1)S(1)}, bf16[1024,128]{1,0:T(8,128)(2,1)S(1)}, u32[]{:S(2)}, u32[]{:S(2)}) collective-permute-start(bf16[1024,128]{1,0:T(8,128)(2,1)S(1)} %get-tuple-element.8.refs_1_), channel_id=1, source_target_pairs={{0,4},{4,0},{1,5},{5,1},{2,6},{6,2},{3,7},{7,3},{8,12},{12,8},{9,1... | collective-permute-start | bytes 786440 | tf_op jit(solution)/shard_map/ppermute | solution.py:188
  44.2 3.4 %collective-permute-start = (bf16[8,272,128]{2,1,0:T(8,128)(2,1)S(1)}, bf16[8,272,128]{2,1,0:T(8,128)(2,1)S(1)}, u32[]{:S(2)}, u32[]{:S(2)}) collective-permute-start(bf16[8,272,128]{2,1,0:T(8,128)(2,1)S(1)} %all_to_all.5.refs_0_), channel_id=1, source_target_pairs={{0,11},{1,8},{2,9},{3,10},{8,19},{9,16},{10,17},{11,18},{16,27},{1... | collective-permute-start | bytes 1671176 | tf_op jit(solution)/shard_map/ppermute | solution.py:191
  47.6 0.0 collective-permute-done.3.refs_1_
  47.6 1.3 %other0.1.refs_2_ = f32[256,1024]{1,0:T(8,128)S(1)} custom-call(bf16[8,272,128]{2,1,0:T(8,128)(2,1)S(1)} %all_to_all.5.refs_0_, bf16[1024,128]{1,0:T(8,128)(2,1)S(1)} %collective-permute-done.3.refs_1_), custom_call_target="tpu_custom_call" | custom-call | flops 1073741824 | bytes 2097152 | tf_op jit(solution)/shard_map/other0/pallas_call | solution.py:115
  49.0 0.0 collective-permute-done.2.refs_0_
  49.0 1.3 %other1.1.refs_2_ = f32[256,1024]{1,0:T(8,128)S(1)} custom-call(bf16[8,272,128]{2,1,0:T(8,128)(2,1)S(1)} %collective-permute-done.2.refs_0_, bf16[1024,128]{1,0:T(8,128)(2,1)S(1)} %collective-permute-done.3.refs_1_, f32[256,1024]{1,0:T(8,128)S(1)} %other0.1.refs_2_), custom_call_target="tpu_custom_call" | custom-call | flops 1073741824 | bytes 2097152 | tf_op jit(solution)/shard_map/other1/pallas_call | solution.py:115
  50.3 0.0 collective-permute-done.1.refs_0_
  50.3 1.3 %other2.1.refs_2_ = f32[256,1024]{1,0:T(8,128)S(1)} custom-call(bf16[8,272,128]{2,1,0:T(8,128)(2,1)S(1)} %collective-permute-done.1.refs_0_, bf16[1024,128]{1,0:T(8,128)(2,1)S(1)} %collective-permute-done.3.refs_1_, f32[256,1024]{1,0:T(8,128)S(1)} %other1.1.refs_2_), custom_call_target="tpu_custom_call" | custom-call | flops 1073741824 | bytes 2097152 | tf_op jit(solution)/shard_map/other2/pallas_call | solution.py:115
  51.7 5.3 %collective-permute-done.refs_0_ = bf16[8,272,128]{2,1,0:T(8,128)(2,1)S(1)} collective-permute-done((bf16[8,272,128]{2,1,0:T(8,128)(2,1)S(1)}, bf16[8,272,128]{2,1,0:T(8,128)(2,1)S(1)}, u32[]{:S(2)}, u32[]{:S(2)}) %collective-permute-start) | collective-permute-done | bytes 557088 | tf_op jit(solution)/shard_map/ppermute | solution.py:191
  56.9 1.3 %other3.1 = bf16[256,1024]{1,0:T(8,128)(2,1)S(1)} custom-call(bf16[8,272,128]{2,1,0:T(8,128)(2,1)S(1)} %collective-permute-done.refs_0_, bf16[1024,128]{1,0:T(8,128)(2,1)S(1)} %collective-permute-done.3.refs_1_, f32[256,1024]{1,0:T(8,128)S(1)} %other2.1.refs_2_), custom_call_target="tpu_custom_call" | custom-call | flops 1073741824 | bytes 2097152 | tf_op jit(solution)/shard_map/other3/pallas_call | solution.py:115
  58.3 4.4 %collective-permute-start.4 = (bf16[256,1024]{1,0:T(8,128)(2,1)S(1)}, bf16[256,1024]{1,0:T(8,128)(2,1)S(1)}, u32[]{:S(2)}, u32[]{:S(2)}) collective-permute-start(bf16[256,1024]{1,0:T(8,128)(2,1)S(1)} %other3.1), channel_id=1, source_target_pairs={{0,4},{4,0},{1,5},{5,1},{2,6},{6,2},{3,7},{7,3},{8,12},{12,8},{9,1... | collective-permute-start | bytes 1572872 | tf_op jit(solution)/shard_map/ppermute | solution.py:200
  64.0 0.1 pad_add_fusion.place_ref
  64.1 1.3 %own0.1.refs_2_ = f32[256,1024]{1,0:T(8,128)S(1)} custom-call(bf16[8,272,128]{2,1,0:T(8,128)(2,1)S(1)} %all_to_all.5.refs_0_, bf16[1024,128]{1,0:T(8,128)(2,1)S(1)} %get-tuple-element.8.refs_1_), custom_call_target="tpu_custom_call" | custom-call | flops 1073741824 | bytes 2097152 | tf_op jit(solution)/shard_map/own0/pallas_call | solution.py:115
  65.4 1.3 %own1.1.refs_2_ = f32[256,1024]{1,0:T(8,128)S(1)} custom-call(bf16[8,272,128]{2,1,0:T(8,128)(2,1)S(1)} %collective-permute-done.2.refs_0_, bf16[1024,128]{1,0:T(8,128)(2,1)S(1)} %get-tuple-element.8.refs_1_, f32[256,1024]{1,0:T(8,128)S(1)} %own0.1.refs_2_), custom_call_target="tpu_custom_call" | custom-call | flops 1073741824 | bytes 2097152 | tf_op jit(solution)/shard_map/own1/pallas_call | solution.py:115
  66.8 1.3 %own2.1.refs_2_ = f32[256,1024]{1,0:T(8,128)S(1)} custom-call(bf16[8,272,128]{2,1,0:T(8,128)(2,1)S(1)} %collective-permute-done.1.refs_0_, bf16[1024,128]{1,0:T(8,128)(2,1)S(1)} %get-tuple-element.8.refs_1_, f32[256,1024]{1,0:T(8,128)S(1)} %own1.1.refs_2_), custom_call_target="tpu_custom_call" | custom-call | flops 1073741824 | bytes 2097152 | tf_op jit(solution)/shard_map/own2/pallas_call | solution.py:115
  68.1 1.3 %own3.1.own_ref = f32[256,1024]{1,0:T(8,128)S(1)} custom-call(bf16[8,272,128]{2,1,0:T(8,128)(2,1)S(1)} %collective-permute-done.refs_0_, bf16[1024,128]{1,0:T(8,128)(2,1)S(1)} %get-tuple-element.8.refs_1_, f32[256,1024]{1,0:T(8,128)S(1)} %own2.1.refs_2_), custom_call_target="tpu_custom_call" | custom-call | flops 1073741824 | bytes 2097152 | tf_op jit(solution)/shard_map/own3/pallas_call | solution.py:115
  69.4 0.0 collective-permute-done.4.other_ref
  69.4 1.7 %finish.1 = f32[256,1024]{1,0:T(8,128)} custom-call(s32[2]{0:T(128)S(1)} %pad_add_fusion.place_ref, f32[256,1024]{1,0:T(8,128)S(1)} %own3.1.own_ref, bf16[256,1024]{1,0:T(8,128)(2,1)S(1)} %collective-permute-done.4.other_ref), custom_call_target="tpu_custom_call" | custom-call | flops 1048576 | bytes 3145728 | tf_op jit(solution)/shard_map/finish/pallas_call | solution.py:140
Async XLA Ops:
  0.0 0.7 copy-start.5
  0.0 0.7 copy-start.3
  0.0 0.7 copy-start.4
  0.7 1.1 %copy-start = (bf16[256,1536]{1,0:T(8,128)(2,1)S(1)}, bf16[256,1536]{1,0:T(8,128)(2,1)}, u32[]{:S(2)}) copy-start(bf16[256,1536]{1,0:T(8,128)(2,1)} %latent_ref.1) | copy-start | bytes 2359300
  1.8 1.0 %copy-start.1 = (bf16[1536,128]{1,0:T(8,128)(2,1)S(1)}, bf16[1536,128]{1,0:T(8,128)(2,1)}, u32[]{:S(2)}) copy-start(bf16[1536,128]{1,0:T(8,128)(2,1)} %weight_ref.1) | copy-start | bytes 1179652
  2.8 0.9 %copy-start.2 = (bf16[1024,128]{1,0:T(8,128)(2,1)S(1)}, bf16[1024,128]{1,0:T(8,128)(2,1)}, u32[]{:S(2)}) copy-start(bf16[1024,128]{1,0:T(8,128)(2,1)} %raw_ref.1) | copy-start | bytes 786436
  35.5 13.5 %collective-permute-start.2 = (bf16[8,272,128]{2,1,0:T(8,128)(2,1)S(1)}, bf16[8,272,128]{2,1,0:T(8,128)(2,1)S(1)}, u32[]{:S(2)}, u32[]{:S(2)}) collective-permute-start(bf16[8,272,128]{2,1,0:T(8,128)(2,1)S(1)} %all_to_all.5.refs_0_), channel_id=1, source_target_pairs={{0,8},{1,9},{2,10},{3,11},{8,16},{9,17},{10,18},{11,19},{16,24},{1... | collective-permute-start | bytes 1671176 | tf_op jit(solution)/shard_map/ppermute | solution.py:189
  37.4 12.9 %collective-permute-start.1 = (bf16[8,272,128]{2,1,0:T(8,128)(2,1)S(1)}, bf16[8,272,128]{2,1,0:T(8,128)(2,1)S(1)}, u32[]{:S(2)}, u32[]{:S(2)}) collective-permute-start(bf16[8,272,128]{2,1,0:T(8,128)(2,1)S(1)} %all_to_all.5.refs_0_), channel_id=1, source_target_pairs={{0,1},{1,2},{2,3},{3,0},{8,9},{9,10},{10,11},{11,8},{16,17},{17,18... | collective-permute-start | bytes 1671176 | tf_op jit(solution)/shard_map/ppermute | solution.py:190
  40.6 7.0 %collective-permute-start.3 = (bf16[1024,128]{1,0:T(8,128)(2,1)S(1)}, bf16[1024,128]{1,0:T(8,128)(2,1)S(1)}, u32[]{:S(2)}, u32[]{:S(2)}) collective-permute-start(bf16[1024,128]{1,0:T(8,128)(2,1)S(1)} %get-tuple-element.8.refs_1_), channel_id=1, source_target_pairs={{0,4},{4,0},{1,5},{5,1},{2,6},{6,2},{3,7},{7,3},{8,12},{12,8},{9,1... | collective-permute-start | bytes 786440 | tf_op jit(solution)/shard_map/ppermute | solution.py:188
  44.2 12.7 %collective-permute-start = (bf16[8,272,128]{2,1,0:T(8,128)(2,1)S(1)}, bf16[8,272,128]{2,1,0:T(8,128)(2,1)S(1)}, u32[]{:S(2)}, u32[]{:S(2)}) collective-permute-start(bf16[8,272,128]{2,1,0:T(8,128)(2,1)S(1)} %all_to_all.5.refs_0_), channel_id=1, source_target_pairs={{0,11},{1,8},{2,9},{3,10},{8,19},{9,16},{10,17},{11,18},{16,27},{1... | collective-permute-start | bytes 1671176 | tf_op jit(solution)/shard_map/ppermute | solution.py:191
  58.3 11.2 %collective-permute-start.4 = (bf16[256,1024]{1,0:T(8,128)(2,1)S(1)}, bf16[256,1024]{1,0:T(8,128)(2,1)S(1)}, u32[]{:S(2)}, u32[]{:S(2)}) collective-permute-start(bf16[256,1024]{1,0:T(8,128)(2,1)S(1)} %other3.1), channel_id=1, source_target_pairs={{0,4},{4,0},{1,5},{5,1},{2,6},{6,2},{3,7},{7,3},{8,12},{12,8},{9,1... | collective-permute-start | bytes 1572872 | tf_op jit(solution)/shard_map/ppermute | solution.py:200

commit v2 on v1

v2 whole, which is shorter than its diff:
```python
import functools

import jax
import jax.numpy as jnp
from jax import lax
from jax.experimental import pallas as pl
from jax.experimental.pallas import tpu as pltpu
from jax.sharding import PartitionSpec as P

VMEM = pltpu.VMEM
HBM = pltpu.HBM
TOKENS = 256
KEYS = 1024
HDIM = 128
ROWS = TOKENS + 16
TB = 32
AHEAD = 6
FLAT = ("ka", "ha")


def front_kernel(
    latent_hbm, weight_hbm, head_hbm, raw_hbm, gain_hbm, bias_hbm,
    block_hbm, keys_hbm,
    latent_ref, weight_ref, head_ref, raw_ref, gain_ref, bias_ref,
    block_ref, keys_ref, sems,
):
    sources = (latent_hbm, weight_hbm, head_hbm, raw_hbm, gain_hbm, bias_hbm)
    targets = (latent_ref, weight_ref, head_ref, raw_ref, gain_ref, bias_ref)
    copies = [
        pltpu.make_async_copy(source, target, sems.at[i])
        for i, (source, target) in enumerate(zip(sources, targets))
    ]
    for copy in copies:
        copy.start()
    for copy in copies[:3]:
        copy.wait()
    block_ref[:TOKENS, :] = jnp.dot(
        latent_ref[...], weight_ref[...], preferred_element_type=jnp.float32
    ).astype(jnp.bfloat16)
    row = head_ref[...].astype(jnp.float32)
    tail_rows = ROWS - TOKENS
    row_at = lax.broadcasted_iota(jnp.int32, (tail_rows, HDIM), 0)
    first = jnp.broadcast_to(row[:, :HDIM], (tail_rows, HDIM))
    second = jnp.broadcast_to(row[:, HDIM:], (tail_rows, HDIM))
    block_ref[TOKENS:, :] = jnp.where(
        row_at == 0, first, jnp.where(row_at == 1, second, 0.0)
    ).astype(jnp.bfloat16)
    outs = []
    for i in range(block_hbm.shape[0]):
        outs.append(pltpu.make_async_copy(block_ref, block_hbm.at[i], sems.at[6 + i]))
        outs[-1].start()
    for copy in copies[3:]:
        copy.wait()
    values = raw_ref[...].astype(jnp.float32)
    center = jnp.mean(values, axis=-1, keepdims=True)
    moved = values - center
    spread = jnp.mean(jnp.square(moved), axis=-1, keepdims=True)
    scaled = moved * lax.rsqrt(spread + 1e-06)
    keys_ref[...] = (scaled * gain_ref[...] + bias_ref[...]).astype(jnp.bfloat16)
    outs.append(pltpu.make_async_copy(keys_ref, keys_hbm, sems.at[0]))
    outs[-1].start()
    for copy in outs:
        copy.wait()


def front(arrays, copies):
    outs = (
        jax.ShapeDtypeStruct((copies, ROWS, HDIM), jnp.bfloat16),
        jax.ShapeDtypeStruct((KEYS, HDIM), jnp.bfloat16),
    )
    return pl.pallas_call(
        front_kernel,
        out_shape=outs,
        in_specs=[pl.BlockSpec(memory_space=HBM)] * len(arrays),
        out_specs=[pl.BlockSpec(memory_space=HBM)] * len(outs),
        scratch_shapes=[VMEM(a.shape, a.dtype) for a in arrays]
        + [VMEM(outs[0].shape[1:], jnp.bfloat16), VMEM(outs[1].shape, jnp.bfloat16)]
        + [pltpu.SemaphoreType.DMA((6 + copies,))],
        compiler_params=pltpu.CompilerParams(vmem_limit_bytes=60 * 2**20),
        cost_estimate=pl.CostEstimate(flops=2 * 256 * 1536 * 128, bytes_accessed=2 * 2**20, transcendentals=1024),
        name="front",
    )(*arrays)


def score_steps(part_refs, keys_refs, total_refs, flush):
    heads = [(p, h) for p in part_refs for h in range(p.shape[0])]
    blocks = TOKENS // TB
    steps = [(k, t, i) for k in range(len(keys_refs)) for t in range(blocks) for i in range(len(heads))]
    slots = AHEAD + 1

    def scoped(*accs):
        def acc(m, s, j):
            return accs[(m * slots + s) * 2 + j]

        zero = jnp.zeros((TB, HDIM), jnp.bfloat16)
        columns = [p[h, TOKENS:, :].astype(jnp.float32).T for p, h in heads]
        for k, keys_ref in enumerate(keys_refs):
            for m in range(2):
                a = keys_ref[512 * m : 512 * m + 256, :]
                b = keys_ref[512 * m + 256 : 512 * m + 512, :]
                pltpu.matmul_push_rhs(jnp.concatenate([a, b], axis=1), k, m, transpose=True)

        def issue(n):
            k, t, i = steps[n]
            p, h = heads[i]
            q = p[h, t * TB : (t + 1) * TB, :]
            low = jnp.concatenate([q, zero], axis=1)
            high = jnp.concatenate([zero, q], axis=1)
            staged = k if t == 0 and i == 0 else None
            for m in range(2):
                pltpu.matmul_acc_lhs(acc(m, n % slots, 0), low, load_staged_rhs=staged)
                pltpu.matmul_acc_lhs(acc(m, n % slots, 1), high)

        for n in range(AHEAD):
            issue(n)
        sums = None
        per_row = HDIM // TB
        for n, (k, t, i) in enumerate(steps):
            if n + AHEAD < len(steps):
                issue(n + AHEAD)
            rows = slice(t * TB, (t + 1) * TB)
            if i == 0:
                if not total_refs:
                    sums = [jnp.zeros((TB, 256), jnp.float32) for _ in range(4)]
                else:
                    sums = [total_refs[k][rows, 256 * g : 256 * (g + 1)] for g in range(4)]
            at = (t % per_row) * TB
            weight = columns[i][at : at + TB, t // per_row : t // per_row + 1]
            weight = jnp.broadcast_to(weight, (TB, 256))
            for m in range(2):
                for j in range(2):
                    score = pltpu.matmul_pop(acc(m, n % slots, j))
                    sums[2 * m + j] = sums[2 * m + j] + jnp.maximum(score, 0.0) * weight
            if i == len(heads) - 1:
                flush(k, t, sums)

    pl.run_scoped(scoped, *[pltpu.ACC(m)((TB, 256), jnp.float32) for m in range(2) for _ in range(2 * slots)])


def score_kernel(*refs, parts, sets, has_totals, has_place):
    if has_place:
        start_ref, order_ref, *refs, reach_ref = refs
        key_begin = (order_ref[...] * lax.axis_size("ha") + lax.axis_index("ha")) * KEYS
        reach_ref[...] = jnp.broadcast_to(start_ref[...] - key_begin, reach_ref.shape)
    part_refs, refs = refs[:parts], refs[parts:]
    keys_refs, refs = refs[:sets], refs[sets:]
    total_refs, out_refs = (refs[:sets], refs[sets:]) if has_totals else ((), refs)

    def flush(k, t, sums):
        rows = slice(t * TB, (t + 1) * TB)
        for g in range(4):
            out_refs[k][rows, 256 * g : 256 * (g + 1)] = sums[g].astype(out_refs[k].dtype)

    score_steps(part_refs, keys_refs, total_refs, flush)


def score_cost(parts, sets):
    heads = sum(p.shape[0] for p in parts)
    return pl.CostEstimate(
        flops=heads * sets * 2**14, bytes_accessed=2**14, transcendentals=0
    )


def scores(parts, keys, totals=(), place=(), out_dtype=jnp.float32, name="scores"):
    operands = (*place, *parts, *keys, *totals)
    outs = [jax.ShapeDtypeStruct((TOKENS, KEYS), out_dtype) for _ in keys]
    if place:
        outs.append(jax.ShapeDtypeStruct((TB, 256), jnp.int32))
    return pl.pallas_call(
        functools.partial(
            score_kernel, parts=len(parts), sets=len(keys), has_totals=bool(totals), has_place=bool(place)
        ),
        out_shape=outs,
        in_specs=[pl.BlockSpec(memory_space=VMEM)] * len(operands),
        out_specs=[pl.BlockSpec(memory_space=VMEM)] * len(outs),
        compiler_params=pltpu.CompilerParams(vmem_limit_bytes=24 * 2**20),
        cost_estimate=score_cost(parts, len(keys)),
        name=name,
    )(*operands)


def finish_kernel(part_ref, keys_ref, total_ref, reach_ref, other_ref, out_hbm, out_ref, sems):
    scale = HDIM ** (-0.5)
    reach = reach_ref[...]
    ahead = lax.broadcasted_iota(jnp.int32, (TB, 256), 1) - lax.broadcasted_iota(jnp.int32, (TB, 256), 0)
    copies = []

    def flush(k, t, sums):
        rows = slice(t * TB, (t + 1) * TB)
        for g in range(4):
            at = slice(256 * g, 256 * (g + 1))
            total = (sums[g] + other_ref[rows, at].astype(jnp.float32)) * scale
            out_ref[rows, at] = jnp.where(ahead <= reach + (t * TB - 256 * g), total, 0.0)
        copies.append(pltpu.make_async_copy(out_ref.at[rows], out_hbm.at[rows], sems.at[t]))
        copies[-1].start()
        if t == TOKENS // TB - 1:
            for copy in copies:
                copy.wait()

    score_steps((part_ref,), (keys_ref,), (total_ref,), flush)


def finish(part, keys, total, reach, other):
    return pl.pallas_call(
        finish_kernel,
        out_shape=jax.ShapeDtypeStruct((TOKENS, KEYS), jnp.float32),
        in_specs=[pl.BlockSpec(memory_space=VMEM)] * 5,
        out_specs=pl.BlockSpec(memory_space=HBM),
        scratch_shapes=[VMEM((TOKENS, KEYS), jnp.float32), pltpu.SemaphoreType.DMA((TOKENS // TB,))],
        compiler_params=pltpu.CompilerParams(vmem_limit_bytes=24 * 2**20),
        cost_estimate=score_cost((part,), 1),
        name="finish",
    )(part, keys, total, reach, other)


def layout(z_size, x_size):
    def flat(z, core, x):
        return ((z % z_size) * 2 + core) * x_size + x % x_size

    sites = [(z, x) for z in range(z_size) for x in range(x_size)]
    groups = [
        [flat(z, core, x) for z, x in sites if (z - x) % x_size == coset]
        for core in range(2)
        for coset in range(x_size)
    ]

    def moved(dz, dx):
        return [
            (flat(z, core, x), flat(z + sign * dz, core, x + sign * dx))
            for core, sign in ((0, 1), (1, -1))
            for z, x in sites
        ]

    swap = [(flat(z, core, x), flat(z, 1 - core, x)) for z, x in sites for core in range(2)]
    return groups, moved, swap


def per_device(
    latent, query_weight, head_weights, raw_keys, key_gain, key_bias, query_start, key_order
):
    ka, ha = lax.axis_size("ka"), lax.axis_size("ha")
    groups, moved, swap = layout(ka // 2, ha)
    block, keys = front(
        (
            latent,
            query_weight,
            head_weights.reshape(1, TOKENS),
            raw_keys,
            key_gain.reshape(1, HDIM),
            key_bias.reshape(1, HDIM),
        ),
        len(groups[0]),
    )
    here = lax.all_to_all(block, FLAT, 0, 0, axis_index_groups=groups)
    diagonal = lax.ppermute(here, FLAT, moved(1, -1))
    along_z = lax.ppermute(here, FLAT, moved(1, 0))
    along_x = lax.ppermute(here, FLAT, moved(0, 1))

    (own,) = scores((here,), (keys,), name="here_own")
    own, swapped = lax.optimization_barrier((own, keys))
    other_keys = lax.ppermute(swapped, FLAT, swap)
    place = (query_start.reshape(1, 1), key_order.reshape(1, 1))
    own, reach = scores((diagonal,), (keys,), (own,), place, name="diagonal_own")
    own, other_keys = lax.optimization_barrier((own, other_keys))
    (other,) = scores((here, diagonal), (other_keys,), name="here_diagonal_other")
    (other,) = scores((along_z,), (other_keys,), (other,), name="z_other")
    (other,) = scores((along_x,), (other_keys,), (other,), out_dtype=jnp.bfloat16, name="x_other")
    received = lax.ppermute(other, FLAT, swap)
    own, other = lax.optimization_barrier((own, other))
    (own,) = scores((along_z,), (keys,), (own,), name="z_own")
    return finish(along_x, keys, own, reach, received)


def solution(mesh):
    in_specs = (
        P("pb", None),
        P(None, ("ka", "ha")),
        P("pb", ("ka", "ha")),
        P(("ka", "ha"), None),
        P(),
        P(),
        P("pb"),
        P("ka"),
    )
    out_specs = P("pb", ("ka", "ha"))
    return jax.shard_map(
        per_device, mesh=mesh, in_specs=in_specs, out_specs=out_specs, check_vma=False
    )
```

time: 71.5 us -> 63.2 us (0.88)
  waiting for transfers between devices: 5.28 us -> 1.27 us
  local copies, waits for them, and re-layouts: 3.77 us -> 0.01 us
  starting transfers between devices: 16.6 us -> 14.5 us
  Pallas kernels: 12.7 us -> 14 us
    ppermute x1, waiting for transfers between devices: 5.27 us -> 0.01 us  [per_device(): diagonal = lax.ppermute(here, FLAT, moved(1, -1))]
    unnamed x12 -> x2, local copies, waits for them, and re-layouts: 3.77 us -> 0.01 us
    ppermute x1, starting transfers between devices: 3.6 us -> 2.08 us  [per_device(): other_keys = lax.ppermute(swapped, FLAT, swap)]
    ppermute x1, starting transfers between devices: 3.4 us -> 1.91 us  [per_device(): diagonal = lax.ppermute(here, FLAT, moved(1, -1))]
    ppermute x1, starting transfers between devices: 4.41 us -> 3.13 us  [per_device(): received = lax.ppermute(other, FLAT, swap)]
    ppermute x1, starting transfers between devices: 1.99 us -> 3.2 us  [per_device(): along_z = lax.ppermute(here, FLAT, moved(1, 0))]
    ppermute x1, waiting for transfers between devices: 0.01 us -> 1.08 us  [per_device(): along_x = lax.ppermute(here, FLAT, moved(0, 1))]
    ppermute x1, starting transfers between devices: 3.16 us -> 4.22 us  [per_device(): along_x = lax.ppermute(here, FLAT, moved(0, 1))]
  transfers between devices with their start and end apart: 5 -> 5, of which waited for: 1 -> 2; matrix products, arithmetic and copies ran while one was open for 0% -> 0% of each run, Pallas kernels for 13% -> 12%
where the time goes in v2:
time: 63.2 us; the launch traced here: 62.9 us
  blocking collectives  31.6 us (50%)
  starting transfers between devices  14.5 us (23%)
  Pallas kernels  14 us (22%)
  between operations  1.43 us (2%)
  waiting for transfers between devices  1.27 us (2%)
    all_to_all x1, blocking collectives, per_device(): here = lax.all_to_all(block, FLAT, 0, 0, axis_index_groups=groups)  31.6 us
    pallas_call x6, Pallas kernels, scores(): pl.pallas_call(functools.partial(score_kernel, parts=len(parts), sets=len...  9.1 us
    ppermute x1, starting transfers between devices, per_device(): along_x = lax.ppermute(here, FLAT, moved(0, 1))  4.22 us
    ppermute x1, starting transfers between devices, per_device(): along_z = lax.ppermute(here, FLAT, moved(1, 0))  3.2 us
    ppermute x1, starting transfers between devices, per_device(): received = lax.ppermute(other, FLAT, swap)  3.13 us
    pallas_call x1, Pallas kernels, front(): pl.pallas_call(front_kernel, out_shape=outs, in_specs=[pl.BlockSpec(memor...  2.79 us
    pallas_call x1, Pallas kernels, finish(): pl.pallas_call(finish_kernel, out_shape=jax.ShapeDtypeStruct((TOKENS, KEY...  2.14 us
    ppermute x1, starting transfers between devices, per_device(): other_keys = lax.ppermute(swapped, FLAT, swap)  2.08 us
  transfers between devices with their start and end apart: 5, of which 2 were waited for; matrix products, arithmetic and copies ran while one was open for 0% of the time, Pallas kernels for 12%

profile of v2, /device:TPU:1, one launch (start us, length us, event | category | flops | bytes accessed | tf_op | source)
XLA Modules:
  0.0 62.9 jit_solution(10529385703480267502)
XLA Ops:
  0.0 2.8 %front.1 = (bf16[8,272,128]{2,1,0:T(8,128)(2,1)}, bf16[1024,128]{1,0:T(8,128)(2,1)}) custom-call(bf16[256,1536]{1,0:T(8,128)(2,1)} %latent_hbm.1, bf16[1536,128]{1,0:T(8,128)(2,1)} %weight_hbm.1, bf16[1,256]{1,0:T(2,128)(2,1)} %bitcast.7, bf16[1024,128]{1,0:T(8,128)(2,1)} %raw_hbm.1, f32[1,128]{1,0:T(1,128)} %bitcast.8, f32[1,128]{1,0:T(1,128)} %bitcast.9), custom_call_target="tpu_custom_call" | custom-call | flops 100663296 | bytes 2097152 | tf_op jit(solution)/shard_map/front/pallas_call | solution.py:71
  2.8 0.0 copy-start
  2.8 31.6 %all_to_all.5.refs_0_ = bf16[8,272,128]{2,1,0:T(8,128)(2,1)S(1)} all-to-all(bf16[8,272,128]{2,1,0:T(8,128)(2,1)} %get-tuple-element.14), channel_id=1, replica_groups={{0,9,18,27,32,41,50,59},{3,8,17,26,35,40,49,58},{2,11,16,25,34,43,48,57..., dimensions={0} | all-to-all | bytes 1114112 | tf_op jit(solution)/shard_map/all_to_all | solution.py:254
  34.4 1.9 %collective-permute-start.2 = (bf16[8,272,128]{2,1,0:T(8,128)(2,1)S(1)}, bf16[8,272,128]{2,1,0:T(8,128)(2,1)S(1)}, u32[]{:S(2)}, u32[]{:S(2)}) collective-permute-start(bf16[8,272,128]{2,1,0:T(8,128)(2,1)S(1)} %all_to_all.5.refs_0_), channel_id=1, source_target_pairs={{0,11},{1,8},{2,9},{3,10},{8,19},{9,16},{10,17},{11,18},{16,27},{1... | collective-permute-start | bytes 1671176 | tf_op jit(solution)/shard_map/ppermute | solution.py:255
  36.3 3.2 %collective-permute-start.1 = (bf16[8,272,128]{2,1,0:T(8,128)(2,1)S(1)}, bf16[8,272,128]{2,1,0:T(8,128)(2,1)S(1)}, u32[]{:S(2)}, u32[]{:S(2)}) collective-permute-start(bf16[8,272,128]{2,1,0:T(8,128)(2,1)S(1)} %all_to_all.5.refs_0_), channel_id=1, source_target_pairs={{0,8},{1,9},{2,10},{3,11},{8,16},{9,17},{10,18},{11,19},{16,24},{1... | collective-permute-start | bytes 1671176 | tf_op jit(solution)/shard_map/ppermute | solution.py:256
  39.5 4.2 %collective-permute-start = (bf16[8,272,128]{2,1,0:T(8,128)(2,1)S(1)}, bf16[8,272,128]{2,1,0:T(8,128)(2,1)S(1)}, u32[]{:S(2)}, u32[]{:S(2)}) collective-permute-start(bf16[8,272,128]{2,1,0:T(8,128)(2,1)S(1)} %all_to_all.5.refs_0_), channel_id=1, source_target_pairs={{0,1},{1,2},{2,3},{3,0},{8,9},{9,10},{10,11},{11,8},{16,17},{17,18... | collective-permute-start | bytes 1671176 | tf_op jit(solution)/shard_map/ppermute | solution.py:257
  43.8 0.0 copy-done
  43.8 1.3 %here_own.1.refs_4_ = f32[256,1024]{1,0:T(8,128)S(1)} custom-call(bf16[8,272,128]{2,1,0:T(8,128)(2,1)S(1)} %all_to_all.5.refs_0_, bf16[1024,128]{1,0:T(8,128)(2,1)S(1)} %copy-done), custom_call_target="tpu_custom_call" | custom-call | flops 131072 | bytes 16384 | tf_op jit(solution)/shard_map/here_own/pallas_call | solution.py:169
  45.1 2.1 %collective-permute-start.3 = (bf16[1024,128]{1,0:T(8,128)(2,1)S(1)}, bf16[1024,128]{1,0:T(8,128)(2,1)S(1)}, u32[]{:S(2)}, u32[]{:S(2)}) collective-permute-start(bf16[1024,128]{1,0:T(8,128)(2,1)S(1)} %copy-done), channel_id=1, source_target_pairs={{0,4},{4,0},{1,5},{5,1},{2,6},{6,2},{3,7},{7,3},{8,12},{12,8},{9,1... | collective-permute-start | bytes 786440 | tf_op jit(solution)/shard_map/ppermute | solution.py:261
  48.5 0.0 collective-permute-done.2.refs_2_.refs_1_
  48.5 1.3 %diagonal_own.1 = (f32[256,1024]{1,0:T(8,128)S(1)}, s32[32,256]{1,0:T(8,128)S(1)}) custom-call(s32[1,1]{1,0:T(1,128)} %bitcast.5.refs_0_, s32[1,1]{1,0:T(1,128)} %bitcast.6.refs_1_, bf16[8,272,128]{2,1,0:T(8,128)(2,1)S(1)} %collective-permute-done.2.refs_2_.refs_1_, bf16[1024,128]{1,0:T(8,128)(2,1)S(1)} %copy-done, f32[256,1024]{1,0:T(8,128)S(1)} %here_own.1.refs_4_), custom_call_target="tpu_custom_call" | custom-call | flops 131072 | bytes 16384 | tf_op jit(solution)/shard_map/diagonal_own/pallas_call | solution.py:169
  49.8 0.0 collective-permute-done.3.refs_2_.refs_1_
  49.8 2.5 %here_diagonal_other.1.refs_2_ = f32[256,1024]{1,0:T(8,128)S(1)} custom-call(bf16[8,272,128]{2,1,0:T(8,128)(2,1)S(1)} %all_to_all.5.refs_0_, bf16[8,272,128]{2,1,0:T(8,128)(2,1)S(1)} %collective-permute-done.2.refs_2_.refs_1_, bf16[1024,128]{1,0:T(8,128)(2,1)S(1)} %collective-permute-done.3.refs_2_.refs_1_), custom_call_target="tpu_custom_call" | custom-call | flops 262144 | bytes 16384 | tf_op jit(solution)/shard_map/here_diagonal_other/pallas_call | solution.py:169
  52.3 0.0 collective-permute-done.1.refs_0_
  52.3 1.3 %z_other.1.refs_2_ = f32[256,1024]{1,0:T(8,128)S(1)} custom-call(bf16[8,272,128]{2,1,0:T(8,128)(2,1)S(1)} %collective-permute-done.1.refs_0_, bf16[1024,128]{1,0:T(8,128)(2,1)S(1)} %collective-permute-done.3.refs_2_.refs_1_, f32[256,1024]{1,0:T(8,128)S(1)} %here_diagonal_other.1.refs_2_), custom_call_target="tpu_custom_call" | custom-call | flops 131072 | bytes 16384 | tf_op jit(solution)/shard_map/z_other/pallas_call | solution.py:169
  53.6 1.1 %collective-permute-done.refs_0_.part_ref = bf16[8,272,128]{2,1,0:T(8,128)(2,1)S(1)} collective-permute-done((bf16[8,272,128]{2,1,0:T(8,128)(2,1)S(1)}, bf16[8,272,128]{2,1,0:T(8,128)(2,1)S(1)}, u32[]{:S(2)}, u32[]{:S(2)}) %collective-permute-start) | collective-permute-done | bytes 557088 | tf_op jit(solution)/shard_map/ppermute | solution.py:257
  54.7 1.3 %x_other.1 = bf16[256,1024]{1,0:T(8,128)(2,1)S(1)} custom-call(bf16[8,272,128]{2,1,0:T(8,128)(2,1)S(1)} %collective-permute-done.refs_0_.part_ref, bf16[1024,128]{1,0:T(8,128)(2,1)S(1)} %collective-permute-done.3.refs_2_.refs_1_, f32[256,1024]{1,0:T(8,128)S(1)} %z_other.1.refs_2_), custom_call_target="tpu_custom_call" | custom-call | flops 131072 | bytes 16384 | tf_op jit(solution)/shard_map/x_other/pallas_call | solution.py:169
  56.1 3.1 %collective-permute-start.4 = (bf16[256,1024]{1,0:T(8,128)(2,1)S(1)}, bf16[256,1024]{1,0:T(8,128)(2,1)S(1)}, u32[]{:S(2)}, u32[]{:S(2)}) collective-permute-start(bf16[256,1024]{1,0:T(8,128)(2,1)S(1)} %x_other.1), channel_id=1, source_target_pairs={{0,4},{4,0},{1,5},{5,1},{2,6},{6,2},{3,7},{7,3},{8,12},{12,8},{9,1... | collective-permute-start | bytes 1572872 | tf_op jit(solution)/shard_map/ppermute | solution.py:268
  59.2 1.3 %z_own.1.total_ref = f32[256,1024]{1,0:T(8,128)S(1)} custom-call(bf16[8,272,128]{2,1,0:T(8,128)(2,1)S(1)} %collective-permute-done.1.refs_0_, bf16[1024,128]{1,0:T(8,128)(2,1)S(1)} %copy-done, f32[256,1024]{1,0:T(8,128)S(1)} %get-tuple-element.21.refs_2_), custom_call_target="tpu_custom_call" | custom-call | flops 131072 | bytes 16384 | tf_op jit(solution)/shard_map/z_own/pallas_call | solution.py:169
  60.5 0.2 collective-permute-done.4.other_ref
  60.7 2.1 %finish.1 = f32[256,1024]{1,0:T(8,128)} custom-call(bf16[8,272,128]{2,1,0:T(8,128)(2,1)S(1)} %collective-permute-done.refs_0_.part_ref, bf16[1024,128]{1,0:T(8,128)(2,1)S(1)} %copy-done, f32[256,1024]{1,0:T(8,128)S(1)} %z_own.1.total_ref, s32[32,256]{1,0:T(8,128)S(1)} %get-tuple-element.22.reach_ref, bf16[256,1024]{1,0:T(8,128)(2,1)S(1)} %collective-permute-done.4.other_ref), custom_call_target="tpu_custom_call" | custom-call | flops 131072 | bytes 16384 | tf_op jit(solution)/shard_map/finish/pallas_call | solution.py:204
Async XLA Ops:
  2.8 41.0 %copy-start = (bf16[1024,128]{1,0:T(8,128)(2,1)S(1)}, bf16[1024,128]{1,0:T(8,128)(2,1)}, u32[]{:S(2)}) copy-start(bf16[1024,128]{1,0:T(8,128)(2,1)} %get-tuple-element.18.refs_1_.refs_3_.keys_ref) | copy-start | bytes 786436
  34.4 14.1 %collective-permute-start.2 = (bf16[8,272,128]{2,1,0:T(8,128)(2,1)S(1)}, bf16[8,272,128]{2,1,0:T(8,128)(2,1)S(1)}, u32[]{:S(2)}, u32[]{:S(2)}) collective-permute-start(bf16[8,272,128]{2,1,0:T(8,128)(2,1)S(1)} %all_to_all.5.refs_0_), channel_id=1, source_target_pairs={{0,11},{1,8},{2,9},{3,10},{8,19},{9,16},{10,17},{11,18},{16,27},{1... | collective-permute-start | bytes 1671176 | tf_op jit(solution)/shard_map/ppermute | solution.py:255
  36.3 16.0 %collective-permute-start.1 = (bf16[8,272,128]{2,1,0:T(8,128)(2,1)S(1)}, bf16[8,272,128]{2,1,0:T(8,128)(2,1)S(1)}, u32[]{:S(2)}, u32[]{:S(2)}) collective-permute-start(bf16[8,272,128]{2,1,0:T(8,128)(2,1)S(1)} %all_to_all.5.refs_0_), channel_id=1, source_target_pairs={{0,8},{1,9},{2,10},{3,11},{8,16},{9,17},{10,18},{11,19},{16,24},{1... | collective-permute-start | bytes 1671176 | tf_op jit(solution)/shard_map/ppermute | solution.py:256
  39.5 15.2 %collective-permute-start = (bf16[8,272,128]{2,1,0:T(8,128)(2,1)S(1)}, bf16[8,272,128]{2,1,0:T(8,128)(2,1)S(1)}, u32[]{:S(2)}, u32[]{:S(2)}) collective-permute-start(bf16[8,272,128]{2,1,0:T(8,128)(2,1)S(1)} %all_to_all.5.refs_0_), channel_id=1, source_target_pairs={{0,1},{1,2},{2,3},{3,0},{8,9},{9,10},{10,11},{11,8},{16,17},{17,18... | collective-permute-start | bytes 1671176 | tf_op jit(solution)/shard_map/ppermute | solution.py:257
  45.1 4.7 %collective-permute-start.3 = (bf16[1024,128]{1,0:T(8,128)(2,1)S(1)}, bf16[1024,128]{1,0:T(8,128)(2,1)S(1)}, u32[]{:S(2)}, u32[]{:S(2)}) collective-permute-start(bf16[1024,128]{1,0:T(8,128)(2,1)S(1)} %copy-done), channel_id=1, source_target_pairs={{0,4},{4,0},{1,5},{5,1},{2,6},{6,2},{3,7},{7,3},{8,12},{12,8},{9,1... | collective-permute-start | bytes 786440 | tf_op jit(solution)/shard_map/ppermute | solution.py:261
  56.1 4.6 %collective-permute-start.4 = (bf16[256,1024]{1,0:T(8,128)(2,1)S(1)}, bf16[256,1024]{1,0:T(8,128)(2,1)S(1)}, u32[]{:S(2)}, u32[]{:S(2)}) collective-permute-start(bf16[256,1024]{1,0:T(8,128)(2,1)S(1)} %x_other.1), channel_id=1, source_target_pairs={{0,4},{4,0},{1,5},{5,1},{2,6},{6,2},{3,7},{7,3},{8,12},{12,8},{9,1... | collective-permute-start | bytes 1572872 | tf_op jit(solution)/shard_map/ppermute | solution.py:268

commit v3 on v2

--- a/solution.py
+++ b/solution.py
@@ -15,17 +15,18 @@
 ROWS = TOKENS + 16
 TB = 32
 AHEAD = 6
+EARLY = 2
 FLAT = ("ka", "ha")
 
 
 def front_kernel(
-    latent_hbm, weight_hbm, head_hbm, raw_hbm, gain_hbm, bias_hbm,
+    raw_hbm, gain_hbm, bias_hbm, latent_hbm, weight_hbm, head_hbm,
     block_hbm, keys_hbm,
-    latent_ref, weight_ref, head_ref, raw_ref, gain_ref, bias_ref,
+    raw_ref, gain_ref, bias_ref, latent_ref, weight_ref, head_ref,
     block_ref, keys_ref, sems,
 ):
-    sources = (latent_hbm, weight_hbm, head_hbm, raw_hbm, gain_hbm, bias_hbm)
-    targets = (latent_ref, weight_ref, head_ref, raw_ref, gain_ref, bias_ref)
+    sources = (raw_hbm, gain_hbm, bias_hbm, latent_hbm, weight_hbm, head_hbm)
+    targets = (raw_ref, gain_ref, bias_ref, latent_ref, weight_ref, head_ref)
     copies = [
         pltpu.make_async_copy(source, target, sems.at[i])
         for i, (source, target) in enumerate(zip(sources, targets))
@@ -34,31 +35,30 @@
         copy.start()
     for copy in copies[:3]:
         copy.wait()
+    values = raw_ref[...].astype(jnp.float32)
+    center = jnp.mean(values, axis=-1, keepdims=True)
+    moved = values - center
+    spread = jnp.mean(jnp.square(moved), axis=-1, keepdims=True)
+    scaled = moved * lax.rsqrt(spread + 1e-06)
+    keys_ref[...] = (scaled * gain_ref[...] + bias_ref[...]).astype(jnp.bfloat16)
+    outs = [pltpu.make_async_copy(keys_ref, keys_hbm, sems.at[0])]
+    outs[-1].start()
+    for copy in copies[3:]:
+        copy.wait()
     block_ref[:TOKENS, :] = jnp.dot(
         latent_ref[...], weight_ref[...], preferred_element_type=jnp.float32
     ).astype(jnp.bfloat16)
     row = head_ref[...].astype(jnp.float32)
     tail_rows = ROWS - TOKENS
     row_at = lax.broadcasted_iota(jnp.int32, (tail_rows, HDIM), 0)
-    first = jnp.broadcast_to(row[:, :HDIM], (tail_rows, HDIM))
-    second = jnp.broadcast_to(row[:, HDIM:], (tail_rows, HDIM))
+    first_row = jnp.broadcast_to(row[:, :HDIM], (tail_rows, HDIM))
+    second_row = jnp.broadcast_to(row[:, HDIM:], (tail_rows, HDIM))
     block_ref[TOKENS:, :] = jnp.where(
-        row_at == 0, first, jnp.where(row_at == 1, second, 0.0)
+        row_at == 0, first_row, jnp.where(row_at == 1, second_row, 0.0)
     ).astype(jnp.bfloat16)
-    outs = []
     for i in range(block_hbm.shape[0]):
         outs.append(pltpu.make_async_copy(block_ref, block_hbm.at[i], sems.at[6 + i]))
         outs[-1].start()
-    for copy in copies[3:]:
-        copy.wait()
-    values = raw_ref[...].astype(jnp.float32)
-    center = jnp.mean(values, axis=-1, keepdims=True)
-    moved = values - center
-    spread = jnp.mean(jnp.square(moved), axis=-1, keepdims=True)
-    scaled = moved * lax.rsqrt(spread + 1e-06)
-    keys_ref[...] = (scaled * gain_ref[...] + bias_ref[...]).astype(jnp.bfloat16)
-    outs.append(pltpu.make_async_copy(keys_ref, keys_hbm, sems.at[0]))
-    outs[-1].start()
     for copy in outs:
         copy.wait()
 
@@ -82,8 +82,9 @@
     )(*arrays)
 
 
-def score_steps(part_refs, keys_refs, total_refs, flush):
-    heads = [(p, h) for p in part_refs for h in range(p.shape[0])]
+def score_steps(part_refs, keys_refs, total_refs, flush, spans=None):
+    spans = spans or [(0, p.shape[0]) for p in part_refs]
+    heads = [(p, h) for p, span in zip(part_refs, spans) for h in range(*span)]
     blocks = TOKENS // TB
     steps = [(k, t, i) for k in range(len(keys_refs)) for t in range(blocks) for i in range(len(heads))]
     slots = AHEAD + 1
@@ -137,11 +138,12 @@
     pl.run_scoped(scoped, *[pltpu.ACC(m)((TB, 256), jnp.float32) for m in range(2) for _ in range(2 * slots)])
 
 
-def score_kernel(*refs, parts, sets, has_totals, has_place):
+def score_kernel(*refs, parts, sets, has_totals, has_place, spans):
     if has_place:
-        start_ref, order_ref, *refs, reach_ref = refs
-        key_begin = (order_ref[...] * lax.axis_size("ha") + lax.axis_index("ha")) * KEYS
-        reach_ref[...] = jnp.broadcast_to(start_ref[...] - key_begin, reach_ref.shape)
+        place_ref, *refs, reach_ref = refs
+        place = place_ref[...]
+        key_begin = (place[:, 1:] * lax.axis_size("ha") + lax.axis_index("ha")) * KEYS
+        reach_ref[...] = jnp.broadcast_to(place[:, :1] - key_begin, reach_ref.shape)
     part_refs, refs = refs[:parts], refs[parts:]
     keys_refs, refs = refs[:sets], refs[sets:]
     total_refs, out_refs = (refs[:sets], refs[sets:]) if has_totals else ((), refs)
@@ -151,7 +153,7 @@
         for g in range(4):
             out_refs[k][rows, 256 * g : 256 * (g + 1)] = sums[g].astype(out_refs[k].dtype)
 
-    score_steps(part_refs, keys_refs, total_refs, flush)
+    score_steps(part_refs, keys_refs, total_refs, flush, spans)
 
 
 def score_cost(parts, sets):
@@ -161,14 +163,19 @@
     )
 
 
-def scores(parts, keys, totals=(), place=(), out_dtype=jnp.float32, name="scores"):
+def scores(parts, keys, totals=(), place=(), out_dtype=jnp.float32, spans=None, name="scores"):
     operands = (*place, *parts, *keys, *totals)
     outs = [jax.ShapeDtypeStruct((TOKENS, KEYS), out_dtype) for _ in keys]
     if place:
         outs.append(jax.ShapeDtypeStruct((TB, 256), jnp.int32))
     return pl.pallas_call(
         functools.partial(
-            score_kernel, parts=len(parts), sets=len(keys), has_totals=bool(totals), has_place=bool(place)
+            score_kernel,
+            parts=len(parts),
+            sets=len(keys),
+            has_totals=bool(totals),
+            has_place=bool(place),
+            spans=spans,
         ),
         out_shape=outs,
         in_specs=[pl.BlockSpec(memory_space=VMEM)] * len(operands),
@@ -197,7 +204,7 @@
             for copy in copies:
                 copy.wait()
 
-    score_steps((part_ref,), (keys_ref,), (total_ref,), flush)
+    score_steps((part_ref,), (keys_ref,), (total_ref,), flush, [(EARLY, part_ref.shape[0])])
 
 
 def finish(part, keys, total, reach, other):
@@ -240,17 +247,9 @@
 ):
     ka, ha = lax.axis_size("ka"), lax.axis_size("ha")
     groups, moved, swap = layout(ka // 2, ha)
-    block, keys = front(
-        (
-            latent,
-            query_weight,
-            head_weights.reshape(1, TOKENS),
-            raw_keys,
-            key_gain.reshape(1, HDIM),
-            key_bias.reshape(1, HDIM),
-        ),
-        len(groups[0]),
-    )
+    gain, bias = key_gain.reshape(1, HDIM), key_bias.reshape(1, HDIM)
+    head_row = head_weights.reshape(1, TOKENS)
+    block, keys = front((raw_keys, gain, bias, latent, query_weight, head_row), len(groups[0]))
     here = lax.all_to_all(block, FLAT, 0, 0, axis_index_groups=groups)
     diagonal = lax.ppermute(here, FLAT, moved(1, -1))
     along_z = lax.ppermute(here, FLAT, moved(1, 0))
@@ -259,7 +258,7 @@
     (own,) = scores((here,), (keys,), name="here_own")
     own, swapped = lax.optimization_barrier((own, keys))
     other_keys = lax.ppermute(swapped, FLAT, swap)
-    place = (query_start.reshape(1, 1), key_order.reshape(1, 1))
+    place = (jnp.concatenate([query_start, key_order]).reshape(1, 2),)
     own, reach = scores((diagonal,), (keys,), (own,), place, name="diagonal_own")
     own, other_keys = lax.optimization_barrier((own, other_keys))
     (other,) = scores((here, diagonal), (other_keys,), name="here_diagonal_other")
@@ -267,7 +266,8 @@
     (other,) = scores((along_x,), (other_keys,), (other,), out_dtype=jnp.bfloat16, name="x_other")
     received = lax.ppermute(other, FLAT, swap)
     own, other = lax.optimization_barrier((own, other))
-    (own,) = scores((along_z,), (keys,), (own,), name="z_own")
+    spans = ((0, along_z.shape[0]), (0, EARLY))
+    (own,) = scores((along_z, along_x), (keys,), (own,), spans=spans, name="z_own")
     return finish(along_x, keys, own, reach, received)
 
 

time: 63.2 us -> 63.1 us (level)
  transfers between devices with their start and end apart: 5 -> 5, of which waited for: 2 -> 1; matrix products, arithmetic and copies ran while one was open for 0% -> 0% of each run, Pallas kernels for 12% -> 13%
where the time goes in v3:
time: 63.1 us; the launch traced here: 62.7 us
  blocking collectives  31.6 us (50%)
  starting transfers between devices  14.5 us (23%)
  Pallas kernels  14 us (22%)
  between operations  1.43 us (2%)
  waiting for transfers between devices  1.03 us (2%)
    all_to_all x1, blocking collectives, per_device(): here = lax.all_to_all(block, FLAT, 0, 0, axis_index_groups=groups)  31.6 us
    pallas_call x6, Pallas kernels, scores(): pl.pallas_call(functools.partial(score_kernel, parts=len(parts), sets=len...  9.41 us
    ppermute x1, starting transfers between devices, per_device(): along_x = lax.ppermute(here, FLAT, moved(0, 1))  4.23 us
    ppermute x1, starting transfers between devices, per_device(): along_z = lax.ppermute(here, FLAT, moved(1, 0))  3.19 us
    ppermute x1, starting transfers between devices, per_device(): received = lax.ppermute(other, FLAT, swap)  3.12 us
    pallas_call x1, Pallas kernels, front(): pl.pallas_call(front_kernel, out_shape=outs, in_specs=[pl.BlockSpec(memor...  2.61 us
    ppermute x1, starting transfers between devices, per_device(): other_keys = lax.ppermute(swapped, FLAT, swap)  2.07 us
    pallas_call x1, Pallas kernels, finish(): pl.pallas_call(finish_kernel, out_shape=jax.ShapeDtypeStruct((TOKENS, KEY...  2.03 us
  transfers between devices with their start and end apart: 5, of which 1 were waited for; matrix products, arithmetic and copies ran while one was open for 0% of the time, Pallas kernels for 13%

profile of v3, /device:TPU:1, one launch (start us, length us, event | category | flops | bytes accessed | tf_op | source)
XLA Modules:
  0.0 62.7 jit_solution(4306948374311711601)
XLA Ops:
  0.0 2.6 %front.1 = (bf16[8,272,128]{2,1,0:T(8,128)(2,1)}, bf16[1024,128]{1,0:T(8,128)(2,1)}) custom-call(bf16[1024,128]{1,0:T(8,128)(2,1)} %raw_hbm.1, f32[1,128]{1,0:T(1,128)} %bitcast.6, f32[1,128]{1,0:T(1,128)} %bitcast.7, bf16[256,1536]{1,0:T(8,128)(2,1)} %latent_hbm.1, bf16[1536,128]{1,0:T(8,128)(2,1)} %weight_hbm.1, bf16[1,256]{1,0:T(2,128)(2,1)} %bitcast.5), custom_call_target="tpu_custom_call" | custom-call | flops 100663296 | bytes 2097152 | tf_op jit(solution)/shard_map/front/pallas_call | solution.py:71
  2.6 0.0 copy-start
  2.6 31.6 %all_to_all.5.refs_0_ = bf16[8,272,128]{2,1,0:T(8,128)(2,1)S(1)} all-to-all(bf16[8,272,128]{2,1,0:T(8,128)(2,1)} %get-tuple-element.14), channel_id=1, replica_groups={{0,9,18,27,32,41,50,59},{3,8,17,26,35,40,49,58},{2,11,16,25,34,43,48,57..., dimensions={0} | all-to-all | bytes 1114112 | tf_op jit(solution)/shard_map/all_to_all | solution.py:253
  34.2 1.9 %collective-permute-start.2 = (bf16[8,272,128]{2,1,0:T(8,128)(2,1)S(1)}, bf16[8,272,128]{2,1,0:T(8,128)(2,1)S(1)}, u32[]{:S(2)}, u32[]{:S(2)}) collective-permute-start(bf16[8,272,128]{2,1,0:T(8,128)(2,1)S(1)} %all_to_all.5.refs_0_), channel_id=1, source_target_pairs={{0,11},{1,8},{2,9},{3,10},{8,19},{9,16},{10,17},{11,18},{16,27},{1... | collective-permute-start | bytes 1671176 | tf_op jit(solution)/shard_map/ppermute | solution.py:254
  36.1 3.2 %collective-permute-start.1 = (bf16[8,272,128]{2,1,0:T(8,128)(2,1)S(1)}, bf16[8,272,128]{2,1,0:T(8,128)(2,1)S(1)}, u32[]{:S(2)}, u32[]{:S(2)}) collective-permute-start(bf16[8,272,128]{2,1,0:T(8,128)(2,1)S(1)} %all_to_all.5.refs_0_), channel_id=1, source_target_pairs={{0,8},{1,9},{2,10},{3,11},{8,16},{9,17},{10,18},{11,19},{16,24},{1... | collective-permute-start | bytes 1671176 | tf_op jit(solution)/shard_map/ppermute | solution.py:255
  39.3 4.2 %collective-permute-start = (bf16[8,272,128]{2,1,0:T(8,128)(2,1)S(1)}, bf16[8,272,128]{2,1,0:T(8,128)(2,1)S(1)}, u32[]{:S(2)}, u32[]{:S(2)}) collective-permute-start(bf16[8,272,128]{2,1,0:T(8,128)(2,1)S(1)} %all_to_all.5.refs_0_), channel_id=1, source_target_pairs={{0,1},{1,2},{2,3},{3,0},{8,9},{9,10},{10,11},{11,8},{16,17},{17,18... | collective-permute-start | bytes 1671176 | tf_op jit(solution)/shard_map/ppermute | solution.py:256
  43.6 0.0 copy-done
  43.6 1.3 %here_own.1.refs_3_ = f32[256,1024]{1,0:T(8,128)S(1)} custom-call(bf16[8,272,128]{2,1,0:T(8,128)(2,1)S(1)} %all_to_all.5.refs_0_, bf16[1024,128]{1,0:T(8,128)(2,1)S(1)} %copy-done), custom_call_target="tpu_custom_call" | custom-call | flops 131072 | bytes 16384 | tf_op jit(solution)/shard_map/here_own/pallas_call | solution.py:171
  44.9 2.1 %collective-permute-start.3 = (bf16[1024,128]{1,0:T(8,128)(2,1)S(1)}, bf16[1024,128]{1,0:T(8,128)(2,1)S(1)}, u32[]{:S(2)}, u32[]{:S(2)}) collective-permute-start(bf16[1024,128]{1,0:T(8,128)(2,1)S(1)} %copy-done), channel_id=1, source_target_pairs={{0,4},{4,0},{1,5},{5,1},{2,6},{6,2},{3,7},{7,3},{8,12},{12,8},{9,1... | collective-permute-start | bytes 786440 | tf_op jit(solution)/shard_map/ppermute | solution.py:260
  48.3 0.1 add_bitcast_fusion.refs_0_
  48.4 0.0 collective-permute-done.2.refs_1_
  48.4 1.3 %diagonal_own.1 = (f32[256,1024]{1,0:T(8,128)S(1)}, s32[32,256]{1,0:T(8,128)S(1)}) custom-call(s32[1,2]{1,0:T(1,128)S(1)} %add_bitcast_fusion.refs_0_, bf16[8,272,128]{2,1,0:T(8,128)(2,1)S(1)} %collective-permute-done.2.refs_1_, bf16[1024,128]{1,0:T(8,128)(2,1)S(1)} %copy-done, f32[256,1024]{1,0:T(8,128)S(1)} %here_own.1.refs_3_), custom_call_target="tpu_custom_call" | custom-call | flops 131072 | bytes 16384 | tf_op jit(solution)/shard_map/diagonal_own/pallas_call | solution.py:171
  49.7 0.0 collective-permute-done.3.refs_2_.refs_1_
  49.7 2.5 %here_diagonal_other.1.refs_2_ = f32[256,1024]{1,0:T(8,128)S(1)} custom-call(bf16[8,272,128]{2,1,0:T(8,128)(2,1)S(1)} %all_to_all.5.refs_0_, bf16[8,272,128]{2,1,0:T(8,128)(2,1)S(1)} %collective-permute-done.2.refs_1_, bf16[1024,128]{1,0:T(8,128)(2,1)S(1)} %collective-permute-done.3.refs_2_.refs_1_), custom_call_target="tpu_custom_call" | custom-call | flops 262144 | bytes 16384 | tf_op jit(solution)/shard_map/here_diagonal_other/pallas_call | solution.py:171
  52.2 0.0 collective-permute-done.1.refs_0_
  52.2 1.3 %z_other.1.refs_2_ = f32[256,1024]{1,0:T(8,128)S(1)} custom-call(bf16[8,272,128]{2,1,0:T(8,128)(2,1)S(1)} %collective-permute-done.1.refs_0_, bf16[1024,128]{1,0:T(8,128)(2,1)S(1)} %collective-permute-done.3.refs_2_.refs_1_, f32[256,1024]{1,0:T(8,128)S(1)} %here_diagonal_other.1.refs_2_), custom_call_target="tpu_custom_call" | custom-call | flops 131072 | bytes 16384 | tf_op jit(solution)/shard_map/z_other/pallas_call | solution.py:171
  53.5 1.0 %collective-permute-done.refs_0_.refs_1_.part_ref = bf16[8,272,128]{2,1,0:T(8,128)(2,1)S(1)} collective-permute-done((bf16[8,272,128]{2,1,0:T(8,128)(2,1)S(1)}, bf16[8,272,128]{2,1,0:T(8,128)(2,1)S(1)}, u32[]{:S(2)}, u32[]{:S(2)}) %collective-permute-start) | collective-permute-done | bytes 557088 | tf_op jit(solution)/shard_map/ppermute | solution.py:256
  54.6 1.3 %x_other.1 = bf16[256,1024]{1,0:T(8,128)(2,1)S(1)} custom-call(bf16[8,272,128]{2,1,0:T(8,128)(2,1)S(1)} %collective-permute-done.refs_0_.refs_1_.part_ref, bf16[1024,128]{1,0:T(8,128)(2,1)S(1)} %collective-permute-done.3.refs_2_.refs_1_, f32[256,1024]{1,0:T(8,128)S(1)} %z_other.1.refs_2_), custom_call_target="tpu_custom_call" | custom-call | flops 131072 | bytes 16384 | tf_op jit(solution)/shard_map/x_other/pallas_call | solution.py:171
  55.9 3.1 %collective-permute-start.4 = (bf16[256,1024]{1,0:T(8,128)(2,1)S(1)}, bf16[256,1024]{1,0:T(8,128)(2,1)S(1)}, u32[]{:S(2)}, u32[]{:S(2)}) collective-permute-start(bf16[256,1024]{1,0:T(8,128)(2,1)S(1)} %x_other.1), channel_id=1, source_target_pairs={{0,4},{4,0},{1,5},{5,1},{2,6},{6,2},{3,7},{7,3},{8,12},{12,8},{9,1... | collective-permute-start | bytes 1572872 | tf_op jit(solution)/shard_map/ppermute | solution.py:267
  59.0 1.6 %z_own.1.total_ref = f32[256,1024]{1,0:T(8,128)S(1)} custom-call(bf16[8,272,128]{2,1,0:T(8,128)(2,1)S(1)} %collective-permute-done.1.refs_0_, bf16[8,272,128]{2,1,0:T(8,128)(2,1)S(1)} %collective-permute-done.refs_0_.refs_1_.part_ref, bf16[1024,128]{1,0:T(8,128)(2,1)S(1)} %copy-done, f32[256,1024]{1,0:T(8,128)S(1)} %get-tuple-element.21.refs_3_), custom_call_target="tpu_custom_call" | custom-call | flops 262144 | bytes 16384 | tf_op jit(solution)/shard_map/z_own/pallas_call | solution.py:171
  60.7 0.0 collective-permute-done.4.other_ref
  60.7 2.0 %finish.1 = f32[256,1024]{1,0:T(8,128)} custom-call(bf16[8,272,128]{2,1,0:T(8,128)(2,1)S(1)} %collective-permute-done.refs_0_.refs_1_.part_ref, bf16[1024,128]{1,0:T(8,128)(2,1)S(1)} %copy-done, f32[256,1024]{1,0:T(8,128)S(1)} %z_own.1.total_ref, s32[32,256]{1,0:T(8,128)S(1)} %get-tuple-element.22.reach_ref, ...), custom_call_target="tpu_custom_call" | custom-call | flops 131072 | bytes 16384 | tf_op jit(solution)/shard_map/finish/pallas_call | solution.py:211
Async XLA Ops:
  2.6 41.0 %copy-start = (bf16[1024,128]{1,0:T(8,128)(2,1)S(1)}, bf16[1024,128]{1,0:T(8,128)(2,1)}, u32[]{:S(2)}) copy-start(bf16[1024,128]{1,0:T(8,128)(2,1)} %get-tuple-element.18.refs_1_.refs_2_.keys_ref) | copy-start | bytes 786436
  34.2 14.2 %collective-permute-start.2 = (bf16[8,272,128]{2,1,0:T(8,128)(2,1)S(1)}, bf16[8,272,128]{2,1,0:T(8,128)(2,1)S(1)}, u32[]{:S(2)}, u32[]{:S(2)}) collective-permute-start(bf16[8,272,128]{2,1,0:T(8,128)(2,1)S(1)} %all_to_all.5.refs_0_), channel_id=1, source_target_pairs={{0,11},{1,8},{2,9},{3,10},{8,19},{9,16},{10,17},{11,18},{16,27},{1... | collective-permute-start | bytes 1671176 | tf_op jit(solution)/shard_map/ppermute | solution.py:254
  36.1 16.1 %collective-permute-start.1 = (bf16[8,272,128]{2,1,0:T(8,128)(2,1)S(1)}, bf16[8,272,128]{2,1,0:T(8,128)(2,1)S(1)}, u32[]{:S(2)}, u32[]{:S(2)}) collective-permute-start(bf16[8,272,128]{2,1,0:T(8,128)(2,1)S(1)} %all_to_all.5.refs_0_), channel_id=1, source_target_pairs={{0,8},{1,9},{2,10},{3,11},{8,16},{9,17},{10,18},{11,19},{16,24},{1... | collective-permute-start | bytes 1671176 | tf_op jit(solution)/shard_map/ppermute | solution.py:255
  39.3 15.2 %collective-permute-start = (bf16[8,272,128]{2,1,0:T(8,128)(2,1)S(1)}, bf16[8,272,128]{2,1,0:T(8,128)(2,1)S(1)}, u32[]{:S(2)}, u32[]{:S(2)}) collective-permute-start(bf16[8,272,128]{2,1,0:T(8,128)(2,1)S(1)} %all_to_all.5.refs_0_), channel_id=1, source_target_pairs={{0,1},{1,2},{2,3},{3,0},{8,9},{9,10},{10,11},{11,8},{16,17},{17,18... | collective-permute-start | bytes 1671176 | tf_op jit(solution)/shard_map/ppermute | solution.py:256
  44.9 4.8 %collective-permute-start.3 = (bf16[1024,128]{1,0:T(8,128)(2,1)S(1)}, bf16[1024,128]{1,0:T(8,128)(2,1)S(1)}, u32[]{:S(2)}, u32[]{:S(2)}) collective-permute-start(bf16[1024,128]{1,0:T(8,128)(2,1)S(1)} %copy-done), channel_id=1, source_target_pairs={{0,4},{4,0},{1,5},{5,1},{2,6},{6,2},{3,7},{7,3},{8,12},{12,8},{9,1... | collective-permute-start | bytes 786440 | tf_op jit(solution)/shard_map/ppermute | solution.py:260
  55.9 4.8 %collective-permute-start.4 = (bf16[256,1024]{1,0:T(8,128)(2,1)S(1)}, bf16[256,1024]{1,0:T(8,128)(2,1)S(1)}, u32[]{:S(2)}, u32[]{:S(2)}) collective-permute-start(bf16[256,1024]{1,0:T(8,128)(2,1)S(1)} %x_other.1), channel_id=1, source_target_pairs={{0,4},{4,0},{1,5},{5,1},{2,6},{6,2},{3,7},{7,3},{8,12},{12,8},{9,1... | collective-permute-start | bytes 1572872 | tf_op jit(solution)/shard_map/ppermute | solution.py:267

commit v4 on v3

--- a/solution.py
+++ b/solution.py
@@ -20,30 +20,17 @@
 
 
 def front_kernel(
-    raw_hbm, gain_hbm, bias_hbm, latent_hbm, weight_hbm, head_hbm,
-    block_hbm, keys_hbm,
-    raw_ref, gain_ref, bias_ref, latent_ref, weight_ref, head_ref,
-    block_ref, keys_ref, sems,
+    latent_hbm, weight_hbm, head_hbm, block_hbm, latent_ref, weight_ref, head_ref, block_ref, sems
 ):
-    sources = (raw_hbm, gain_hbm, bias_hbm, latent_hbm, weight_hbm, head_hbm)
-    targets = (raw_ref, gain_ref, bias_ref, latent_ref, weight_ref, head_ref)
+    sources = (latent_hbm, weight_hbm, head_hbm)
+    targets = (latent_ref, weight_ref, head_ref)
     copies = [
         pltpu.make_async_copy(source, target, sems.at[i])
         for i, (source, target) in enumerate(zip(sources, targets))
     ]
     for copy in copies:
         copy.start()
-    for copy in copies[:3]:
-        copy.wait()
-    values = raw_ref[...].astype(jnp.float32)
-    center = jnp.mean(values, axis=-1, keepdims=True)
-    moved = values - center
-    spread = jnp.mean(jnp.square(moved), axis=-1, keepdims=True)
-    scaled = moved * lax.rsqrt(spread + 1e-06)
-    keys_ref[...] = (scaled * gain_ref[...] + bias_ref[...]).astype(jnp.bfloat16)
-    outs = [pltpu.make_async_copy(keys_ref, keys_hbm, sems.at[0])]
-    outs[-1].start()
-    for copy in copies[3:]:
+    for copy in copies:
         copy.wait()
     block_ref[:TOKENS, :] = jnp.dot(
         latent_ref[...], weight_ref[...], preferred_element_type=jnp.float32
@@ -51,31 +38,27 @@
     row = head_ref[...].astype(jnp.float32)
     tail_rows = ROWS - TOKENS
     row_at = lax.broadcasted_iota(jnp.int32, (tail_rows, HDIM), 0)
-    first_row = jnp.broadcast_to(row[:, :HDIM], (tail_rows, HDIM))
-    second_row = jnp.broadcast_to(row[:, HDIM:], (tail_rows, HDIM))
+    first = jnp.broadcast_to(row[:, :HDIM], (tail_rows, HDIM))
+    second = jnp.broadcast_to(row[:, HDIM:], (tail_rows, HDIM))
     block_ref[TOKENS:, :] = jnp.where(
-        row_at == 0, first_row, jnp.where(row_at == 1, second_row, 0.0)
+        row_at == 0, first, jnp.where(row_at == 1, second, 0.0)
     ).astype(jnp.bfloat16)
+    outs = []
     for i in range(block_hbm.shape[0]):
-        outs.append(pltpu.make_async_copy(block_ref, block_hbm.at[i], sems.at[6 + i]))
+        outs.append(pltpu.make_async_copy(block_ref, block_hbm.at[i], sems.at[i]))
         outs[-1].start()
     for copy in outs:
         copy.wait()
 
 
 def front(arrays, copies):
-    outs = (
-        jax.ShapeDtypeStruct((copies, ROWS, HDIM), jnp.bfloat16),
-        jax.ShapeDtypeStruct((KEYS, HDIM), jnp.bfloat16),
-    )
     return pl.pallas_call(
         front_kernel,
-        out_shape=outs,
+        out_shape=jax.ShapeDtypeStruct((copies, ROWS, HDIM), jnp.bfloat16),
         in_specs=[pl.BlockSpec(memory_space=HBM)] * len(arrays),
-        out_specs=[pl.BlockSpec(memory_space=HBM)] * len(outs),
+        out_specs=pl.BlockSpec(memory_space=HBM),
         scratch_shapes=[VMEM(a.shape, a.dtype) for a in arrays]
-        + [VMEM(outs[0].shape[1:], jnp.bfloat16), VMEM(outs[1].shape, jnp.bfloat16)]
-        + [pltpu.SemaphoreType.DMA((6 + copies,))],
+        + [VMEM((ROWS, HDIM), jnp.bfloat16), pltpu.SemaphoreType.DMA((max(copies, len(arrays)),))],
         compiler_params=pltpu.CompilerParams(vmem_limit_bytes=60 * 2**20),
         cost_estimate=pl.CostEstimate(flops=2 * 256 * 1536 * 128, bytes_accessed=2 * 2**20, transcendentals=1024),
         name="front",
@@ -138,12 +121,41 @@
     pl.run_scoped(scoped, *[pltpu.ACC(m)((TB, 256), jnp.float32) for m in range(2) for _ in range(2 * slots)])
 
 
+def first_kernel(part_ref, raw_ref, gain_ref, bias_ref, total_ref, keys_ref):
+    values = raw_ref[...].astype(jnp.float32)
+    center = jnp.mean(values, axis=-1, keepdims=True)
+    moved = values - center
+    spread = jnp.mean(jnp.square(moved), axis=-1, keepdims=True)
+    scaled = moved * lax.rsqrt(spread + 1e-06)
+    keys_ref[...] = (scaled * gain_ref[...] + bias_ref[...]).astype(jnp.bfloat16)
+
+    def flush(k, t, sums):
+        for g in range(4):
+            total_ref[t * TB : (t + 1) * TB, 256 * g : 256 * (g + 1)] = sums[g]
+
+    score_steps((part_ref,), (keys_ref,), (), flush)
+
+
+def first(part, raw_keys, gain, bias):
+    return pl.pallas_call(
+        first_kernel,
+        out_shape=(
+            jax.ShapeDtypeStruct((TOKENS, KEYS), jnp.float32),
+            jax.ShapeDtypeStruct((KEYS, HDIM), jnp.bfloat16),
+        ),
+        in_specs=[pl.BlockSpec(memory_space=VMEM)] * 4,
+        out_specs=[pl.BlockSpec(memory_space=VMEM)] * 2,
+        compiler_params=pltpu.CompilerParams(vmem_limit_bytes=24 * 2**20),
+        cost_estimate=score_cost((part,), 1),
+        name="here_own",
+    )(part, raw_keys, gain, bias)
+
+
 def score_kernel(*refs, parts, sets, has_totals, has_place, spans):
     if has_place:
-        place_ref, *refs, reach_ref = refs
-        place = place_ref[...]
-        key_begin = (place[:, 1:] * lax.axis_size("ha") + lax.axis_index("ha")) * KEYS
-        reach_ref[...] = jnp.broadcast_to(place[:, :1] - key_begin, reach_ref.shape)
+        start_ref, order_ref, *refs, reach_ref = refs
+        key_begin = (order_ref[...] * lax.axis_size("ha") + lax.axis_index("ha")) * KEYS
+        reach_ref[...] = jnp.broadcast_to(start_ref[...] - key_begin, reach_ref.shape)
     part_refs, refs = refs[:parts], refs[parts:]
     keys_refs, refs = refs[:sets], refs[sets:]
     total_refs, out_refs = (refs[:sets], refs[sets:]) if has_totals else ((), refs)
@@ -247,18 +259,16 @@
 ):
     ka, ha = lax.axis_size("ka"), lax.axis_size("ha")
     groups, moved, swap = layout(ka // 2, ha)
-    gain, bias = key_gain.reshape(1, HDIM), key_bias.reshape(1, HDIM)
-    head_row = head_weights.reshape(1, TOKENS)
-    block, keys = front((raw_keys, gain, bias, latent, query_weight, head_row), len(groups[0]))
+    block = front((latent, query_weight, head_weights.reshape(1, TOKENS)), len(groups[0]))
     here = lax.all_to_all(block, FLAT, 0, 0, axis_index_groups=groups)
     diagonal = lax.ppermute(here, FLAT, moved(1, -1))
     along_z = lax.ppermute(here, FLAT, moved(1, 0))
     along_x = lax.ppermute(here, FLAT, moved(0, 1))
 
-    (own,) = scores((here,), (keys,), name="here_own")
+    own, keys = first(here, raw_keys, key_gain.reshape(1, HDIM), key_bias.reshape(1, HDIM))
     own, swapped = lax.optimization_barrier((own, keys))
     other_keys = lax.ppermute(swapped, FLAT, swap)
-    place = (jnp.concatenate([query_start, key_order]).reshape(1, 2),)
+    place = (query_start.reshape(1, 1), key_order.reshape(1, 1))
     own, reach = scores((diagonal,), (keys,), (own,), place, name="diagonal_own")
     own, other_keys = lax.optimization_barrier((own, other_keys))
     (other,) = scores((here, diagonal), (other_keys,), name="here_diagonal_other")

time: 63.1 us -> 62.9 us (level)
  waiting for transfers between devices: 1.03 us -> 0.08 us
  local copies, waits for them, and re-layouts: 0.01 us -> 0.65 us
    pallas_call x1 -> x2, Pallas kernels: 2.61 us -> 4.12 us  [the longest x1 2.45 us: front(): pl.pallas_call(front_kernel, out_shape=jax.ShapeDtypeStruct((copies, ROWS...]
    pallas_call x6 -> x5, Pallas kernels: 9.41 us -> 8.07 us  [scores(): pl.pallas_call(functools.partial(score_kernel, parts=len(parts), sets=len...]
    ppermute x1, waiting for transfers between devices: 1.02 us -> 0.07 us  [per_device(): along_x = lax.ppermute(here, FLAT, moved(0, 1))]
    unnamed x2 -> x6, local copies, waits for them, and re-layouts: 0.01 us -> 0.65 us
where the time goes in v4:
time: 62.9 us; the launch traced here: 62.5 us
  blocking collectives  31.6 us (50%)
  starting transfers between devices  14.5 us (23%)
  Pallas kernels  14.2 us (23%)
  between operations  1.45 us (2%)
  local copies, waits for them, and re-layouts  0.65 us (1%)
    all_to_all x1, blocking collectives, per_device(): here = lax.all_to_all(block, FLAT, 0, 0, axis_index_groups=groups)  31.6 us
    pallas_call x5, Pallas kernels, scores(): pl.pallas_call(functools.partial(score_kernel, parts=len(parts), sets=len...  8.07 us
    ppermute x1, starting transfers between devices, per_device(): along_x = lax.ppermute(here, FLAT, moved(0, 1))  4.22 us
    ppermute x1, starting transfers between devices, per_device(): along_z = lax.ppermute(here, FLAT, moved(1, 0))  3.2 us
    ppermute x1, starting transfers between devices, per_device(): received = lax.ppermute(other, FLAT, swap)  3.12 us
    pallas_call x1, Pallas kernels, front(): pl.pallas_call(front_kernel, out_shape=jax.ShapeDtypeStruct((copies, ROWS...  2.45 us
    ppermute x1, starting transfers between devices, per_device(): other_keys = lax.ppermute(swapped, FLAT, swap)  2.07 us
    pallas_call x1, Pallas kernels, finish(): pl.pallas_call(finish_kernel, out_shape=jax.ShapeDtypeStruct((TOKENS, KEY...  2.03 us
  transfers between devices with their start and end apart: 5, of which 1 were waited for; matrix products, arithmetic and copies ran while one was open for 0% of the time, Pallas kernels for 13%

profile of v4, /device:TPU:1, one launch (start us, length us, event | category | flops | bytes accessed | tf_op | source)
XLA Modules:
  0.0 62.5 jit_solution(17161303237100445979)
XLA Ops:
  0.0 2.4 %front.1 = bf16[8,272,128]{2,1,0:T(8,128)(2,1)} custom-call(bf16[256,1536]{1,0:T(8,128)(2,1)} %latent_hbm.1, bf16[1536,128]{1,0:T(8,128)(2,1)} %weight_hbm.1, bf16[1,256]{1,0:T(2,128)(2,1)} %bitcast.9), custom_call_target="tpu_custom_call" | custom-call | flops 100663296 | bytes 2097152 | tf_op jit(solution)/shard_map/front/pallas_call | solution.py:55
  2.5 0.0 copy-start
  2.5 31.6 %all_to_all.5.part_ref.refs_0_ = bf16[8,272,128]{2,1,0:T(8,128)(2,1)S(1)} all-to-all(bf16[8,272,128]{2,1,0:T(8,128)(2,1)} %front.1), channel_id=1, replica_groups={{0,9,18,27,32,41,50,59},{3,8,17,26,35,40,49,58},{2,11,16,25,34,43,48,57..., dimensions={0} | all-to-all | bytes 1114112 | tf_op jit(solution)/shard_map/all_to_all | solution.py:263
  34.1 1.9 %collective-permute-start.2 = (bf16[8,272,128]{2,1,0:T(8,128)(2,1)S(1)}, bf16[8,272,128]{2,1,0:T(8,128)(2,1)S(1)}, u32[]{:S(2)}, u32[]{:S(2)}) collective-permute-start(bf16[8,272,128]{2,1,0:T(8,128)(2,1)S(1)} %all_to_all.5.part_ref.refs_0_), channel_id=1, source_target_pairs={{0,11},{1,8},{2,9},{3,10},{8,19},{9,16},{10,17},{11,18},{16,27},{1... | collective-permute-start | bytes 1671176 | tf_op jit(solution)/shard_map/ppermute | solution.py:264
  36.0 3.2 %collective-permute-start.1 = (bf16[8,272,128]{2,1,0:T(8,128)(2,1)S(1)}, bf16[8,272,128]{2,1,0:T(8,128)(2,1)S(1)}, u32[]{:S(2)}, u32[]{:S(2)}) collective-permute-start(bf16[8,272,128]{2,1,0:T(8,128)(2,1)S(1)} %all_to_all.5.part_ref.refs_0_), channel_id=1, source_target_pairs={{0,8},{1,9},{2,10},{3,11},{8,16},{9,17},{10,18},{11,19},{16,24},{1... | collective-permute-start | bytes 1671176 | tf_op jit(solution)/shard_map/ppermute | solution.py:265
  39.2 4.2 %collective-permute-start = (bf16[8,272,128]{2,1,0:T(8,128)(2,1)S(1)}, bf16[8,272,128]{2,1,0:T(8,128)(2,1)S(1)}, u32[]{:S(2)}, u32[]{:S(2)}) collective-permute-start(bf16[8,272,128]{2,1,0:T(8,128)(2,1)S(1)} %all_to_all.5.part_ref.refs_0_), channel_id=1, source_target_pairs={{0,1},{1,2},{2,3},{3,0},{8,9},{9,10},{10,11},{11,8},{16,17},{17,18... | collective-permute-start | bytes 1671176 | tf_op jit(solution)/shard_map/ppermute | solution.py:266
  43.4 0.0 copy-start.1
  43.4 0.0 copy-start.2
  43.4 0.0 copy-done
  43.5 0.6 copy-done.1
  44.1 0.0 copy-done.2
  44.1 1.7 %here_own.1 = (f32[256,1024]{1,0:T(8,128)S(1)}, bf16[1024,128]{1,0:T(8,128)(2,1)S(1)}) custom-call(bf16[8,272,128]{2,1,0:T(8,128)(2,1)S(1)} %all_to_all.5.part_ref.refs_0_, bf16[1024,128]{1,0:T(8,128)(2,1)S(1)} %copy-done, f32[1,128]{1,0:T(1,128)S(1)} %bitcast.7, f32[1,128]{1,0:T(1,128)S(1)} %bitcast.8), custom_call_target="tpu_custom_call" | custom-call | flops 131072 | bytes 16384 | tf_op jit(solution)/shard_map/here_own/pallas_call | solution.py:140
  45.8 2.1 %collective-permute-start.3 = (bf16[1024,128]{1,0:T(8,128)(2,1)S(1)}, bf16[1024,128]{1,0:T(8,128)(2,1)S(1)}, u32[]{:S(2)}, u32[]{:S(2)}) collective-permute-start(bf16[1024,128]{1,0:T(8,128)(2,1)S(1)} %get-tuple-element.13.refs_3_.refs_2_.keys_ref), channel_id=1, source_target_pairs={{0,4},{4,0},{1,5},{5,1},{2,6},{6,2},{3,7},{7,3},{8,12},{12,8},{9,1... | collective-permute-start | bytes 786440 | tf_op jit(solution)/shard_map/ppermute | solution.py:270
  49.2 0.0 collective-permute-done.2.refs_2_.refs_1_
  49.2 1.3 %diagonal_own.1 = (f32[256,1024]{1,0:T(8,128)S(1)}, s32[32,256]{1,0:T(8,128)S(1)}) custom-call(s32[1,1]{1,0:T(1,128)} %bitcast.5.refs_0_, s32[1,1]{1,0:T(1,128)} %bitcast.6.refs_1_, bf16[8,272,128]{2,1,0:T(8,128)(2,1)S(1)} %collective-permute-done.2.refs_2_.refs_1_, bf16[1024,128]{1,0:T(8,128)(2,1)S(1)} %get-tuple-element.13.refs_3_.refs_2_.keys_ref, ...), custom_call_target="tpu_custom_call" | custom-call | flops 131072 | bytes 16384 | tf_op jit(solution)/shard_map/diagonal_own/pallas_call | solution.py:183
  50.5 0.0 collective-permute-done.3.refs_2_.refs_1_
  50.5 2.5 %here_diagonal_other.1.refs_2_ = f32[256,1024]{1,0:T(8,128)S(1)} custom-call(bf16[8,272,128]{2,1,0:T(8,128)(2,1)S(1)} %all_to_all.5.part_ref.refs_0_, bf16[8,272,128]{2,1,0:T(8,128)(2,1)S(1)} %collective-permute-done.2.refs_2_.refs_1_, bf16[1024,128]{1,0:T(8,128)(2,1)S(1)} %collective-permute-done.3.refs_2_.refs_1_), custom_call_target="tpu_custom_call" | custom-call | flops 262144 | bytes 16384 | tf_op jit(solution)/shard_map/here_diagonal_other/pallas_call | solution.py:183
  53.0 0.0 collective-permute-done.1.refs_0_
  53.0 1.3 %z_other.1.refs_2_ = f32[256,1024]{1,0:T(8,128)S(1)} custom-call(bf16[8,272,128]{2,1,0:T(8,128)(2,1)S(1)} %collective-permute-done.1.refs_0_, bf16[1024,128]{1,0:T(8,128)(2,1)S(1)} %collective-permute-done.3.refs_2_.refs_1_, f32[256,1024]{1,0:T(8,128)S(1)} %here_diagonal_other.1.refs_2_), custom_call_target="tpu_custom_call" | custom-call | flops 131072 | bytes 16384 | tf_op jit(solution)/shard_map/z_other/pallas_call | solution.py:183
  54.3 0.1 collective-permute-done.refs_0_.refs_1_.part_ref
  54.4 1.3 %x_other.1 = bf16[256,1024]{1,0:T(8,128)(2,1)S(1)} custom-call(bf16[8,272,128]{2,1,0:T(8,128)(2,1)S(1)} %collective-permute-done.refs_0_.refs_1_.part_ref, bf16[1024,128]{1,0:T(8,128)(2,1)S(1)} %collective-permute-done.3.refs_2_.refs_1_, f32[256,1024]{1,0:T(8,128)S(1)} %z_other.1.refs_2_), custom_call_target="tpu_custom_call" | custom-call | flops 131072 | bytes 16384 | tf_op jit(solution)/shard_map/x_other/pallas_call | solution.py:183
  55.7 3.1 %collective-permute-start.4 = (bf16[256,1024]{1,0:T(8,128)(2,1)S(1)}, bf16[256,1024]{1,0:T(8,128)(2,1)S(1)}, u32[]{:S(2)}, u32[]{:S(2)}) collective-permute-start(bf16[256,1024]{1,0:T(8,128)(2,1)S(1)} %x_other.1), channel_id=1, source_target_pairs={{0,4},{4,0},{1,5},{5,1},{2,6},{6,2},{3,7},{7,3},{8,12},{12,8},{9,1... | collective-permute-start | bytes 1572872 | tf_op jit(solution)/shard_map/ppermute | solution.py:277
  58.9 1.6 %z_own.1.total_ref = f32[256,1024]{1,0:T(8,128)S(1)} custom-call(bf16[8,272,128]{2,1,0:T(8,128)(2,1)S(1)} %collective-permute-done.1.refs_0_, bf16[8,272,128]{2,1,0:T(8,128)(2,1)S(1)} %collective-permute-done.refs_0_.refs_1_.part_ref, bf16[1024,128]{1,0:T(8,128)(2,1)S(1)} %get-tuple-element.13.refs_3_.refs_2_.keys_ref, f32[256,1024]{1,0:T(8,128)S(1)} %get-tuple-element.19.refs_3_), custom_call_target="tpu_custom_call" | custom-call | flops 262144 | bytes 16384 | tf_op jit(solution)/shard_map/z_own/pallas_call | solution.py:183
  60.5 0.0 collective-permute-done.4.other_ref
  60.5 2.0 %finish.1 = f32[256,1024]{1,0:T(8,128)} custom-call(bf16[8,272,128]{2,1,0:T(8,128)(2,1)S(1)} %collective-permute-done.refs_0_.refs_1_.part_ref, bf16[1024,128]{1,0:T(8,128)(2,1)S(1)} %get-tuple-element.13.refs_3_.refs_2_.keys_ref, f32[256,1024]{1,0:T(8,128)S(1)} %z_own.1.total_ref, s32[32,256]{1,0:T(8,128)S(1)} %get-tuple-element.20.reach_ref, ...), custom_call_target="tpu_custom_call" | custom-call | flops 131072 | bytes 16384 | tf_op jit(solution)/shard_map/finish/pallas_call | solution.py:223
Async XLA Ops:
  2.5 41.0 %copy-start = (bf16[1024,128]{1,0:T(8,128)(2,1)S(1)}, bf16[1024,128]{1,0:T(8,128)(2,1)}, u32[]{:S(2)}) copy-start(bf16[1024,128]{1,0:T(8,128)(2,1)} %raw_ref.1) | copy-start | bytes 786436
  34.1 15.1 %collective-permute-start.2 = (bf16[8,272,128]{2,1,0:T(8,128)(2,1)S(1)}, bf16[8,272,128]{2,1,0:T(8,128)(2,1)S(1)}, u32[]{:S(2)}, u32[]{:S(2)}) collective-permute-start(bf16[8,272,128]{2,1,0:T(8,128)(2,1)S(1)} %all_to_all.5.part_ref.refs_0_), channel_id=1, source_target_pairs={{0,11},{1,8},{2,9},{3,10},{8,19},{9,16},{10,17},{11,18},{16,27},{1... | collective-permute-start | bytes 1671176 | tf_op jit(solution)/shard_map/ppermute | solution.py:264
  36.0 17.0 %collective-permute-start.1 = (bf16[8,272,128]{2,1,0:T(8,128)(2,1)S(1)}, bf16[8,272,128]{2,1,0:T(8,128)(2,1)S(1)}, u32[]{:S(2)}, u32[]{:S(2)}) collective-permute-start(bf16[8,272,128]{2,1,0:T(8,128)(2,1)S(1)} %all_to_all.5.part_ref.refs_0_), channel_id=1, source_target_pairs={{0,8},{1,9},{2,10},{3,11},{8,16},{9,17},{10,18},{11,19},{16,24},{1... | collective-permute-start | bytes 1671176 | tf_op jit(solution)/shard_map/ppermute | solution.py:265
  39.2 15.2 %collective-permute-start = (bf16[8,272,128]{2,1,0:T(8,128)(2,1)S(1)}, bf16[8,272,128]{2,1,0:T(8,128)(2,1)S(1)}, u32[]{:S(2)}, u32[]{:S(2)}) collective-permute-start(bf16[8,272,128]{2,1,0:T(8,128)(2,1)S(1)} %all_to_all.5.part_ref.refs_0_), channel_id=1, source_target_pairs={{0,1},{1,2},{2,3},{3,0},{8,9},{9,10},{10,11},{11,8},{16,17},{17,18... | collective-permute-start | bytes 1671176 | tf_op jit(solution)/shard_map/ppermute | solution.py:266
  43.4 0.7 %copy-start.1 = (f32[128]{0:T(128)S(1)}, f32[128]{0:T(128)}, u32[]{:S(2)}) copy-start(f32[128]{0:T(128)} %param.12) | copy-start | bytes 1540
  43.4 0.7 %copy-start.2 = (f32[128]{0:T(128)S(1)}, f32[128]{0:T(128)}, u32[]{:S(2)}) copy-start(f32[128]{0:T(128)} %param.13) | copy-start | bytes 1540
  45.8 4.7 %collective-permute-start.3 = (bf16[1024,128]{1,0:T(8,128)(2,1)S(1)}, bf16[1024,128]{1,0:T(8,128)(2,1)S(1)}, u32[]{:S(2)}, u32[]{:S(2)}) collective-permute-start(bf16[1024,128]{1,0:T(8,128)(2,1)S(1)} %get-tuple-element.13.refs_3_.refs_2_.keys_ref), channel_id=1, source_target_pairs={{0,4},{4,0},{1,5},{5,1},{2,6},{6,2},{3,7},{7,3},{8,12},{12,8},{9,1... | collective-permute-start | bytes 786440 | tf_op jit(solution)/shard_map/ppermute | solution.py:270
  55.7 4.8 %collective-permute-start.4 = (bf16[256,1024]{1,0:T(8,128)(2,1)S(1)}, bf16[256,1024]{1,0:T(8,128)(2,1)S(1)}, u32[]{:S(2)}, u32[]{:S(2)}) collective-permute-start(bf16[256,1024]{1,0:T(8,128)(2,1)S(1)} %x_other.1), channel_id=1, source_target_pairs={{0,4},{4,0},{1,5},{5,1},{2,6},{6,2},{3,7},{7,3},{8,12},{12,8},{9,1... | collective-permute-start | bytes 1572872 | tf_op jit(solution)/shard_map/ppermute | solution.py:277

commit v5 on v4

--- a/solution.py
+++ b/solution.py
@@ -268,16 +268,15 @@
     own, keys = first(here, raw_keys, key_gain.reshape(1, HDIM), key_bias.reshape(1, HDIM))
     own, swapped = lax.optimization_barrier((own, keys))
     other_keys = lax.ppermute(swapped, FLAT, swap)
-    place = (query_start.reshape(1, 1), key_order.reshape(1, 1))
-    own, reach = scores((diagonal,), (keys,), (own,), place, name="diagonal_own")
+    (own,) = scores((diagonal,), (keys,), (own,), name="diagonal_own")
     own, other_keys = lax.optimization_barrier((own, other_keys))
     (other,) = scores((here, diagonal), (other_keys,), name="here_diagonal_other")
-    (other,) = scores((along_z,), (other_keys,), (other,), name="z_other")
+    other, own = scores((along_z,), (other_keys, keys), (other, own), name="z_both")
     (other,) = scores((along_x,), (other_keys,), (other,), out_dtype=jnp.bfloat16, name="x_other")
     received = lax.ppermute(other, FLAT, swap)
     own, other = lax.optimization_barrier((own, other))
-    spans = ((0, along_z.shape[0]), (0, EARLY))
-    (own,) = scores((along_z, along_x), (keys,), (own,), spans=spans, name="z_own")
+    place = (query_start.reshape(1, 1), key_order.reshape(1, 1))
+    own, reach = scores((along_x,), (keys,), (own,), place, spans=((0, EARLY),), name="x_early")
     return finish(along_x, keys, own, reach, received)
 
 

time: 62.9 us -> 64.2 us (1.021)
  starting transfers between devices: 14.5 us -> 15.6 us
    ppermute x1, starting transfers between devices: 3.12 us -> 4.22 us  [per_device(): received = lax.ppermute(other, FLAT, swap)]
where the time goes in v5:
time: 64.2 us; the launch traced here: 63.8 us
  blocking collectives  31.6 us (49%)
  starting transfers between devices  15.6 us (24%)
  Pallas kernels  14.2 us (22%)
  between operations  1.45 us (2%)
  local copies, waits for them, and re-layouts  0.65 us (1%)
    all_to_all x1, blocking collectives, per_device(): here = lax.all_to_all(block, FLAT, 0, 0, axis_index_groups=groups)  31.6 us
    pallas_call x5, Pallas kernels, scores(): pl.pallas_call(functools.partial(score_kernel, parts=len(parts), sets=len...  8.04 us
    ppermute x1, starting transfers between devices, per_device(): along_x = lax.ppermute(here, FLAT, moved(0, 1))  4.22 us
    ppermute x1, starting transfers between devices, per_device(): received = lax.ppermute(other, FLAT, swap)  4.22 us
    ppermute x1, starting transfers between devices, per_device(): along_z = lax.ppermute(here, FLAT, moved(1, 0))  3.2 us
    pallas_call x1, Pallas kernels, front(): pl.pallas_call(front_kernel, out_shape=jax.ShapeDtypeStruct((copies, ROWS...  2.45 us
    ppermute x1, starting transfers between devices, per_device(): other_keys = lax.ppermute(swapped, FLAT, swap)  2.07 us
    pallas_call x1, Pallas kernels, finish(): pl.pallas_call(finish_kernel, out_shape=jax.ShapeDtypeStruct((TOKENS, KEY...  2.03 us
  transfers between devices with their start and end apart: 5, of which 1 were waited for; matrix products, arithmetic and copies ran while one was open for 0% of the time, Pallas kernels for 13%

profile of v5, /device:TPU:1, one launch (start us, length us, event | category | flops | bytes accessed | tf_op | source)
XLA Modules:
  0.0 63.8 jit_solution(10072755316702700348)
XLA Ops:
  0.0 2.4 %front.1 = bf16[8,272,128]{2,1,0:T(8,128)(2,1)} custom-call(bf16[256,1536]{1,0:T(8,128)(2,1)} %latent_hbm.1, bf16[1536,128]{1,0:T(8,128)(2,1)} %weight_hbm.1, bf16[1,256]{1,0:T(2,128)(2,1)} %bitcast.9), custom_call_target="tpu_custom_call" | custom-call | flops 100663296 | bytes 2097152 | tf_op jit(solution)/shard_map/front/pallas_call | solution.py:55
  2.5 0.0 copy-start
  2.5 31.6 %all_to_all.5.part_ref.refs_0_ = bf16[8,272,128]{2,1,0:T(8,128)(2,1)S(1)} all-to-all(bf16[8,272,128]{2,1,0:T(8,128)(2,1)} %front.1), channel_id=1, replica_groups={{0,9,18,27,32,41,50,59},{3,8,17,26,35,40,49,58},{2,11,16,25,34,43,48,57..., dimensions={0} | all-to-all | bytes 1114112 | tf_op jit(solution)/shard_map/all_to_all | solution.py:263
  34.1 1.9 %collective-permute-start.2 = (bf16[8,272,128]{2,1,0:T(8,128)(2,1)S(1)}, bf16[8,272,128]{2,1,0:T(8,128)(2,1)S(1)}, u32[]{:S(2)}, u32[]{:S(2)}) collective-permute-start(bf16[8,272,128]{2,1,0:T(8,128)(2,1)S(1)} %all_to_all.5.part_ref.refs_0_), channel_id=1, source_target_pairs={{0,11},{1,8},{2,9},{3,10},{8,19},{9,16},{10,17},{11,18},{16,27},{1... | collective-permute-start | bytes 1671176 | tf_op jit(solution)/shard_map/ppermute | solution.py:264
  36.0 3.2 %collective-permute-start.1 = (bf16[8,272,128]{2,1,0:T(8,128)(2,1)S(1)}, bf16[8,272,128]{2,1,0:T(8,128)(2,1)S(1)}, u32[]{:S(2)}, u32[]{:S(2)}) collective-permute-start(bf16[8,272,128]{2,1,0:T(8,128)(2,1)S(1)} %all_to_all.5.part_ref.refs_0_), channel_id=1, source_target_pairs={{0,8},{1,9},{2,10},{3,11},{8,16},{9,17},{10,18},{11,19},{16,24},{1... | collective-permute-start | bytes 1671176 | tf_op jit(solution)/shard_map/ppermute | solution.py:265
  39.2 4.2 %collective-permute-start = (bf16[8,272,128]{2,1,0:T(8,128)(2,1)S(1)}, bf16[8,272,128]{2,1,0:T(8,128)(2,1)S(1)}, u32[]{:S(2)}, u32[]{:S(2)}) collective-permute-start(bf16[8,272,128]{2,1,0:T(8,128)(2,1)S(1)} %all_to_all.5.part_ref.refs_0_), channel_id=1, source_target_pairs={{0,1},{1,2},{2,3},{3,0},{8,9},{9,10},{10,11},{11,8},{16,17},{17,18... | collective-permute-start | bytes 1671176 | tf_op jit(solution)/shard_map/ppermute | solution.py:266
  43.4 0.0 copy-start.1
  43.4 0.0 copy-start.2
  43.4 0.0 copy-done
  43.5 0.6 copy-done.1
  44.1 0.0 copy-done.2
  44.1 1.7 %here_own.1 = (f32[256,1024]{1,0:T(8,128)S(1)}, bf16[1024,128]{1,0:T(8,128)(2,1)S(1)}) custom-call(bf16[8,272,128]{2,1,0:T(8,128)(2,1)S(1)} %all_to_all.5.part_ref.refs_0_, bf16[1024,128]{1,0:T(8,128)(2,1)S(1)} %copy-done, f32[1,128]{1,0:T(1,128)S(1)} %bitcast.7, f32[1,128]{1,0:T(1,128)S(1)} %bitcast.8), custom_call_target="tpu_custom_call" | custom-call | flops 131072 | bytes 16384 | tf_op jit(solution)/shard_map/here_own/pallas_call | solution.py:140
  45.8 2.1 %collective-permute-start.3 = (bf16[1024,128]{1,0:T(8,128)(2,1)S(1)}, bf16[1024,128]{1,0:T(8,128)(2,1)S(1)}, u32[]{:S(2)}, u32[]{:S(2)}) collective-permute-start(bf16[1024,128]{1,0:T(8,128)(2,1)S(1)} %get-tuple-element.15.refs_1_.refs_2_.refs_3_.keys_ref), channel_id=1, source_target_pairs={{0,4},{4,0},{1,5},{5,1},{2,6},{6,2},{3,7},{7,3},{8,12},{12,8},{9,1... | collective-permute-start | bytes 786440 | tf_op jit(solution)/shard_map/ppermute | solution.py:270
  47.9 0.0 collective-permute-done.2.refs_0_.refs_1_
  47.9 1.3 %diagonal_own.1.refs_4_ = f32[256,1024]{1,0:T(8,128)S(1)} custom-call(bf16[8,272,128]{2,1,0:T(8,128)(2,1)S(1)} %collective-permute-done.2.refs_0_.refs_1_, bf16[1024,128]{1,0:T(8,128)(2,1)S(1)} %get-tuple-element.15.refs_1_.refs_2_.refs_3_.keys_ref, f32[256,1024]{1,0:T(8,128)S(1)} %get-tuple-element.16.refs_2_), custom_call_target="tpu_custom_call" | custom-call | flops 131072 | bytes 16384 | tf_op jit(solution)/shard_map/diagonal_own/pallas_call | solution.py:183
  49.2 0.0 collective-permute-done.3.refs_2_.refs_1_
  49.2 2.5 %here_diagonal_other.1.refs_3_ = f32[256,1024]{1,0:T(8,128)S(1)} custom-call(bf16[8,272,128]{2,1,0:T(8,128)(2,1)S(1)} %all_to_all.5.part_ref.refs_0_, bf16[8,272,128]{2,1,0:T(8,128)(2,1)S(1)} %collective-permute-done.2.refs_0_.refs_1_, bf16[1024,128]{1,0:T(8,128)(2,1)S(1)} %collective-permute-done.3.refs_2_.refs_1_), custom_call_target="tpu_custom_call" | custom-call | flops 262144 | bytes 16384 | tf_op jit(solution)/shard_map/here_diagonal_other/pallas_call | solution.py:183
  51.7 0.0 collective-permute-done.1.refs_0_
  51.7 2.4 %z_both.1 = (f32[256,1024]{1,0:T(8,128)S(1)}, f32[256,1024]{1,0:T(8,128)S(1)}) custom-call(bf16[8,272,128]{2,1,0:T(8,128)(2,1)S(1)} %collective-permute-done.1.refs_0_, bf16[1024,128]{1,0:T(8,128)(2,1)S(1)} %collective-permute-done.3.refs_2_.refs_1_, bf16[1024,128]{1,0:T(8,128)(2,1)S(1)} %get-tuple-element.15.refs_1_.refs_2_.refs_3_.keys_ref, ...), custom_call_target="tpu_custom_call" | custom-call | flops 262144 | bytes 16384 | tf_op jit(solution)/shard_map/z_both/pallas_call | solution.py:183
  54.1 0.3 collective-permute-done.refs_0_.refs_2_.part_ref
  54.4 1.3 %x_other.1 = bf16[256,1024]{1,0:T(8,128)(2,1)S(1)} custom-call(bf16[8,272,128]{2,1,0:T(8,128)(2,1)S(1)} %collective-permute-done.refs_0_.refs_2_.part_ref, bf16[1024,128]{1,0:T(8,128)(2,1)S(1)} %collective-permute-done.3.refs_2_.refs_1_, f32[256,1024]{1,0:T(8,128)S(1)} %get-tuple-element.21.refs_2_), custom_call_target="tpu_custom_call" | custom-call | flops 131072 | bytes 16384 | tf_op jit(solution)/shard_map/x_other/pallas_call | solution.py:183
  55.7 4.2 %collective-permute-start.4 = (bf16[256,1024]{1,0:T(8,128)(2,1)S(1)}, bf16[256,1024]{1,0:T(8,128)(2,1)S(1)}, u32[]{:S(2)}, u32[]{:S(2)}) collective-permute-start(bf16[256,1024]{1,0:T(8,128)(2,1)S(1)} %x_other.1), channel_id=1, source_target_pairs={{0,4},{4,0},{1,5},{5,1},{2,6},{6,2},{3,7},{7,3},{8,12},{12,8},{9,1... | collective-permute-start | bytes 1572872 | tf_op jit(solution)/shard_map/ppermute | solution.py:276
  61.2 0.5 x_early.1
  61.8 0.0 collective-permute-done.4.other_ref
  61.8 2.0 %finish.1 = f32[256,1024]{1,0:T(8,128)} custom-call(bf16[8,272,128]{2,1,0:T(8,128)(2,1)S(1)} %collective-permute-done.refs_0_.refs_2_.part_ref, bf16[1024,128]{1,0:T(8,128)(2,1)S(1)} %get-tuple-element.15.refs_1_.refs_2_.refs_3_.keys_ref, f32[256,1024]{1,0:T(8,128)S(1)} %get-tuple-element.23.total_ref, s32[32,256]{1,0:T(8,128)S(1)} %get-tuple-element.24.reach_ref, ...), custom_call_target="tpu_custom_call" | custom-call | flops 131072 | bytes 16384 | tf_op jit(solution)/shard_map/finish/pallas_call | solution.py:223
Async XLA Ops:
  2.5 41.0 %copy-start = (bf16[1024,128]{1,0:T(8,128)(2,1)S(1)}, bf16[1024,128]{1,0:T(8,128)(2,1)}, u32[]{:S(2)}) copy-start(bf16[1024,128]{1,0:T(8,128)(2,1)} %raw_ref.1) | copy-start | bytes 786436
  34.1 13.8 %collective-permute-start.2 = (bf16[8,272,128]{2,1,0:T(8,128)(2,1)S(1)}, bf16[8,272,128]{2,1,0:T(8,128)(2,1)S(1)}, u32[]{:S(2)}, u32[]{:S(2)}) collective-permute-start(bf16[8,272,128]{2,1,0:T(8,128)(2,1)S(1)} %all_to_all.5.part_ref.refs_0_), channel_id=1, source_target_pairs={{0,11},{1,8},{2,9},{3,10},{8,19},{9,16},{10,17},{11,18},{16,27},{1... | collective-permute-start | bytes 1671176 | tf_op jit(solution)/shard_map/ppermute | solution.py:264
  36.0 15.7 %collective-permute-start.1 = (bf16[8,272,128]{2,1,0:T(8,128)(2,1)S(1)}, bf16[8,272,128]{2,1,0:T(8,128)(2,1)S(1)}, u32[]{:S(2)}, u32[]{:S(2)}) collective-permute-start(bf16[8,272,128]{2,1,0:T(8,128)(2,1)S(1)} %all_to_all.5.part_ref.refs_0_), channel_id=1, source_target_pairs={{0,8},{1,9},{2,10},{3,11},{8,16},{9,17},{10,18},{11,19},{16,24},{1... | collective-permute-start | bytes 1671176 | tf_op jit(solution)/shard_map/ppermute | solution.py:265
  39.2 15.2 %collective-permute-start = (bf16[8,272,128]{2,1,0:T(8,128)(2,1)S(1)}, bf16[8,272,128]{2,1,0:T(8,128)(2,1)S(1)}, u32[]{:S(2)}, u32[]{:S(2)}) collective-permute-start(bf16[8,272,128]{2,1,0:T(8,128)(2,1)S(1)} %all_to_all.5.part_ref.refs_0_), channel_id=1, source_target_pairs={{0,1},{1,2},{2,3},{3,0},{8,9},{9,10},{10,11},{11,8},{16,17},{17,18... | collective-permute-start | bytes 1671176 | tf_op jit(solution)/shard_map/ppermute | solution.py:266
  43.4 0.7 %copy-start.1 = (f32[128]{0:T(128)S(1)}, f32[128]{0:T(128)}, u32[]{:S(2)}) copy-start(f32[128]{0:T(128)} %param.12) | copy-start | bytes 1540
  43.4 0.7 %copy-start.2 = (f32[128]{0:T(128)S(1)}, f32[128]{0:T(128)}, u32[]{:S(2)}) copy-start(f32[128]{0:T(128)} %param.13) | copy-start | bytes 1540
  45.8 3.4 %collective-permute-start.3 = (bf16[1024,128]{1,0:T(8,128)(2,1)S(1)}, bf16[1024,128]{1,0:T(8,128)(2,1)S(1)}, u32[]{:S(2)}, u32[]{:S(2)}) collective-permute-start(bf16[1024,128]{1,0:T(8,128)(2,1)S(1)} %get-tuple-element.15.refs_1_.refs_2_.refs_3_.keys_ref), channel_id=1, source_target_pairs={{0,4},{4,0},{1,5},{5,1},{2,6},{6,2},{3,7},{7,3},{8,12},{12,8},{9,1... | collective-permute-start | bytes 786440 | tf_op jit(solution)/shard_map/ppermute | solution.py:270
  55.7 6.0 %collective-permute-start.4 = (bf16[256,1024]{1,0:T(8,128)(2,1)S(1)}, bf16[256,1024]{1,0:T(8,128)(2,1)S(1)}, u32[]{:S(2)}, u32[]{:S(2)}) collective-permute-start(bf16[256,1024]{1,0:T(8,128)(2,1)S(1)} %x_other.1), channel_id=1, source_target_pairs={{0,4},{4,0},{1,5},{5,1},{2,6},{6,2},{3,7},{7,3},{8,12},{12,8},{9,1... | collective-permute-start | bytes 1572872 | tf_op jit(solution)/shard_map/ppermute | solution.py:276

commit v6 on v4

--- a/solution.py
+++ b/solution.py
@@ -22,19 +22,14 @@
 def front_kernel(
     latent_hbm, weight_hbm, head_hbm, block_hbm, latent_ref, weight_ref, head_ref, block_ref, sems
 ):
-    sources = (latent_hbm, weight_hbm, head_hbm)
-    targets = (latent_ref, weight_ref, head_ref)
-    copies = [
-        pltpu.make_async_copy(source, target, sems.at[i])
-        for i, (source, target) in enumerate(zip(sources, targets))
-    ]
+    half = TOKENS // 2
+    pairs = [(weight_hbm, weight_ref), (head_hbm, head_ref)]
+    pairs += [(latent_hbm.at[pl.ds(i * half, half)], latent_ref.at[pl.ds(i * half, half)]) for i in range(2)]
+    copies = [pltpu.make_async_copy(source, target, sems.at[i]) for i, (source, target) in enumerate(pairs)]
     for copy in copies:
         copy.start()
-    for copy in copies:
+    for copy in copies[:2]:
         copy.wait()
-    block_ref[:TOKENS, :] = jnp.dot(
-        latent_ref[...], weight_ref[...], preferred_element_type=jnp.float32
-    ).astype(jnp.bfloat16)
     row = head_ref[...].astype(jnp.float32)
     tail_rows = ROWS - TOKENS
     row_at = lax.broadcasted_iota(jnp.int32, (tail_rows, HDIM), 0)
@@ -44,9 +39,17 @@
         row_at == 0, first, jnp.where(row_at == 1, second, 0.0)
     ).astype(jnp.bfloat16)
     outs = []
-    for i in range(block_hbm.shape[0]):
-        outs.append(pltpu.make_async_copy(block_ref, block_hbm.at[i], sems.at[i]))
-        outs[-1].start()
+    for i in range(2):
+        copies[2 + i].wait()
+        rows = slice(i * half, (i + 1) * half)
+        block_ref[rows, :] = jnp.dot(
+            latent_ref[rows, :], weight_ref[...], preferred_element_type=jnp.float32
+        ).astype(jnp.bfloat16)
+        part = pl.ds(i * half, half if i == 0 else ROWS - half)
+        for n in range(block_hbm.shape[0]):
+            sem = sems.at[4 + i * block_hbm.shape[0] + n]
+            outs.append(pltpu.make_async_copy(block_ref.at[part], block_hbm.at[n, part], sem))
+            outs[-1].start()
     for copy in outs:
         copy.wait()
 
@@ -58,7 +61,7 @@
         in_specs=[pl.BlockSpec(memory_space=HBM)] * len(arrays),
         out_specs=pl.BlockSpec(memory_space=HBM),
         scratch_shapes=[VMEM(a.shape, a.dtype) for a in arrays]
-        + [VMEM((ROWS, HDIM), jnp.bfloat16), pltpu.SemaphoreType.DMA((max(copies, len(arrays)),))],
+        + [VMEM((ROWS, HDIM), jnp.bfloat16), pltpu.SemaphoreType.DMA((4 + 2 * copies,))],
         compiler_params=pltpu.CompilerParams(vmem_limit_bytes=60 * 2**20),
         cost_estimate=pl.CostEstimate(flops=2 * 256 * 1536 * 128, bytes_accessed=2 * 2**20, transcendentals=1024),
         name="front",

time: 62.9 us -> 63 us (level)
  no operation moved by 1% of the time
where the time goes in v6:
time: 63 us; the launch traced here: 62.6 us
  blocking collectives  31.6 us (50%)
  starting transfers between devices  14.5 us (23%)
  Pallas kernels  14.3 us (23%)
  between operations  1.45 us (2%)
  local copies, waits for them, and re-layouts  0.65 us (1%)
    all_to_all x1, blocking collectives, per_device(): here = lax.all_to_all(block, FLAT, 0, 0, axis_index_groups=groups)  31.6 us
    pallas_call x5, Pallas kernels, scores(): pl.pallas_call(functools.partial(score_kernel, parts=len(parts), sets=len...  8.07 us
    ppermute x1, starting transfers between devices, per_device(): along_x = lax.ppermute(here, FLAT, moved(0, 1))  4.23 us
    ppermute x1, starting transfers between devices, per_device(): along_z = lax.ppermute(here, FLAT, moved(1, 0))  3.19 us
    ppermute x1, starting transfers between devices, per_device(): received = lax.ppermute(other, FLAT, swap)  3.12 us
    pallas_call x1, Pallas kernels, front(): pl.pallas_call(front_kernel, out_shape=jax.ShapeDtypeStruct((copies, ROWS...  2.52 us
    ppermute x1, starting transfers between devices, per_device(): other_keys = lax.ppermute(swapped, FLAT, swap)  2.08 us
    pallas_call x1, Pallas kernels, finish(): pl.pallas_call(finish_kernel, out_shape=jax.ShapeDtypeStruct((TOKENS, KEY...  2.03 us
  transfers between devices with their start and end apart: 5, of which 1 were waited for; matrix products, arithmetic and copies ran while one was open for 0% of the time, Pallas kernels for 13%

profile of v6, /device:TPU:1, one launch (start us, length us, event | category | flops | bytes accessed | tf_op | source)
XLA Modules:
  0.0 62.6 jit_solution(14706258937874078274)
XLA Ops:
  0.0 2.5 %front.1 = bf16[8,272,128]{2,1,0:T(8,128)(2,1)} custom-call(bf16[256,1536]{1,0:T(8,128)(2,1)} %latent_hbm.1, bf16[1536,128]{1,0:T(8,128)(2,1)} %weight_hbm.1, bf16[1,256]{1,0:T(2,128)(2,1)} %bitcast.9), custom_call_target="tpu_custom_call" | custom-call | flops 100663296 | bytes 2097152 | tf_op jit(solution)/shard_map/front/pallas_call | solution.py:58
  2.5 0.0 copy-start
  2.5 31.6 %all_to_all.5.part_ref.refs_0_ = bf16[8,272,128]{2,1,0:T(8,128)(2,1)S(1)} all-to-all(bf16[8,272,128]{2,1,0:T(8,128)(2,1)} %front.1), channel_id=1, replica_groups={{0,9,18,27,32,41,50,59},{3,8,17,26,35,40,49,58},{2,11,16,25,34,43,48,57..., dimensions={0} | all-to-all | bytes 1114112 | tf_op jit(solution)/shard_map/all_to_all | solution.py:266
  34.1 1.9 %collective-permute-start.2 = (bf16[8,272,128]{2,1,0:T(8,128)(2,1)S(1)}, bf16[8,272,128]{2,1,0:T(8,128)(2,1)S(1)}, u32[]{:S(2)}, u32[]{:S(2)}) collective-permute-start(bf16[8,272,128]{2,1,0:T(8,128)(2,1)S(1)} %all_to_all.5.part_ref.refs_0_), channel_id=1, source_target_pairs={{0,11},{1,8},{2,9},{3,10},{8,19},{9,16},{10,17},{11,18},{16,27},{1... | collective-permute-start | bytes 1671176 | tf_op jit(solution)/shard_map/ppermute | solution.py:267
  36.1 3.2 %collective-permute-start.1 = (bf16[8,272,128]{2,1,0:T(8,128)(2,1)S(1)}, bf16[8,272,128]{2,1,0:T(8,128)(2,1)S(1)}, u32[]{:S(2)}, u32[]{:S(2)}) collective-permute-start(bf16[8,272,128]{2,1,0:T(8,128)(2,1)S(1)} %all_to_all.5.part_ref.refs_0_), channel_id=1, source_target_pairs={{0,8},{1,9},{2,10},{3,11},{8,16},{9,17},{10,18},{11,19},{16,24},{1... | collective-permute-start | bytes 1671176 | tf_op jit(solution)/shard_map/ppermute | solution.py:268
  39.3 4.2 %collective-permute-start = (bf16[8,272,128]{2,1,0:T(8,128)(2,1)S(1)}, bf16[8,272,128]{2,1,0:T(8,128)(2,1)S(1)}, u32[]{:S(2)}, u32[]{:S(2)}) collective-permute-start(bf16[8,272,128]{2,1,0:T(8,128)(2,1)S(1)} %all_to_all.5.part_ref.refs_0_), channel_id=1, source_target_pairs={{0,1},{1,2},{2,3},{3,0},{8,9},{9,10},{10,11},{11,8},{16,17},{17,18... | collective-permute-start | bytes 1671176 | tf_op jit(solution)/shard_map/ppermute | solution.py:269
  43.5 0.0 copy-start.1
  43.5 0.0 copy-start.2
  43.5 0.0 copy-done
  43.5 0.6 copy-done.1
  44.1 0.0 copy-done.2
  44.2 1.7 %here_own.1 = (f32[256,1024]{1,0:T(8,128)S(1)}, bf16[1024,128]{1,0:T(8,128)(2,1)S(1)}) custom-call(bf16[8,272,128]{2,1,0:T(8,128)(2,1)S(1)} %all_to_all.5.part_ref.refs_0_, bf16[1024,128]{1,0:T(8,128)(2,1)S(1)} %copy-done, f32[1,128]{1,0:T(1,128)S(1)} %bitcast.7, f32[1,128]{1,0:T(1,128)S(1)} %bitcast.8), custom_call_target="tpu_custom_call" | custom-call | flops 131072 | bytes 16384 | tf_op jit(solution)/shard_map/here_own/pallas_call | solution.py:143
  45.8 2.1 %collective-permute-start.3 = (bf16[1024,128]{1,0:T(8,128)(2,1)S(1)}, bf16[1024,128]{1,0:T(8,128)(2,1)S(1)}, u32[]{:S(2)}, u32[]{:S(2)}) collective-permute-start(bf16[1024,128]{1,0:T(8,128)(2,1)S(1)} %get-tuple-element.13.refs_3_.refs_2_.keys_ref), channel_id=1, source_target_pairs={{0,4},{4,0},{1,5},{5,1},{2,6},{6,2},{3,7},{7,3},{8,12},{12,8},{9,1... | collective-permute-start | bytes 786440 | tf_op jit(solution)/shard_map/ppermute | solution.py:273
  49.2 0.0 collective-permute-done.2.refs_2_.refs_1_
  49.2 1.3 %diagonal_own.1 = (f32[256,1024]{1,0:T(8,128)S(1)}, s32[32,256]{1,0:T(8,128)S(1)}) custom-call(s32[1,1]{1,0:T(1,128)} %bitcast.5.refs_0_, s32[1,1]{1,0:T(1,128)} %bitcast.6.refs_1_, bf16[8,272,128]{2,1,0:T(8,128)(2,1)S(1)} %collective-permute-done.2.refs_2_.refs_1_, bf16[1024,128]{1,0:T(8,128)(2,1)S(1)} %get-tuple-element.13.refs_3_.refs_2_.keys_ref, ...), custom_call_target="tpu_custom_call" | custom-call | flops 131072 | bytes 16384 | tf_op jit(solution)/shard_map/diagonal_own/pallas_call | solution.py:186
  50.6 0.0 collective-permute-done.3.refs_2_.refs_1_
  50.6 2.5 %here_diagonal_other.1.refs_2_ = f32[256,1024]{1,0:T(8,128)S(1)} custom-call(bf16[8,272,128]{2,1,0:T(8,128)(2,1)S(1)} %all_to_all.5.part_ref.refs_0_, bf16[8,272,128]{2,1,0:T(8,128)(2,1)S(1)} %collective-permute-done.2.refs_2_.refs_1_, bf16[1024,128]{1,0:T(8,128)(2,1)S(1)} %collective-permute-done.3.refs_2_.refs_1_), custom_call_target="tpu_custom_call" | custom-call | flops 262144 | bytes 16384 | tf_op jit(solution)/shard_map/here_diagonal_other/pallas_call | solution.py:186
  53.0 0.0 collective-permute-done.1.refs_0_
  53.1 1.3 %z_other.1.refs_2_ = f32[256,1024]{1,0:T(8,128)S(1)} custom-call(bf16[8,272,128]{2,1,0:T(8,128)(2,1)S(1)} %collective-permute-done.1.refs_0_, bf16[1024,128]{1,0:T(8,128)(2,1)S(1)} %collective-permute-done.3.refs_2_.refs_1_, f32[256,1024]{1,0:T(8,128)S(1)} %here_diagonal_other.1.refs_2_), custom_call_target="tpu_custom_call" | custom-call | flops 131072 | bytes 16384 | tf_op jit(solution)/shard_map/z_other/pallas_call | solution.py:186
  54.4 0.1 collective-permute-done.refs_0_.refs_1_.part_ref
  54.5 1.3 %x_other.1 = bf16[256,1024]{1,0:T(8,128)(2,1)S(1)} custom-call(bf16[8,272,128]{2,1,0:T(8,128)(2,1)S(1)} %collective-permute-done.refs_0_.refs_1_.part_ref, bf16[1024,128]{1,0:T(8,128)(2,1)S(1)} %collective-permute-done.3.refs_2_.refs_1_, f32[256,1024]{1,0:T(8,128)S(1)} %z_other.1.refs_2_), custom_call_target="tpu_custom_call" | custom-call | flops 131072 | bytes 16384 | tf_op jit(solution)/shard_map/x_other/pallas_call | solution.py:186
  55.8 3.1 %collective-permute-start.4 = (bf16[256,1024]{1,0:T(8,128)(2,1)S(1)}, bf16[256,1024]{1,0:T(8,128)(2,1)S(1)}, u32[]{:S(2)}, u32[]{:S(2)}) collective-permute-start(bf16[256,1024]{1,0:T(8,128)(2,1)S(1)} %x_other.1), channel_id=1, source_target_pairs={{0,4},{4,0},{1,5},{5,1},{2,6},{6,2},{3,7},{7,3},{8,12},{12,8},{9,1... | collective-permute-start | bytes 1572872 | tf_op jit(solution)/shard_map/ppermute | solution.py:280
  58.9 1.6 %z_own.1.total_ref = f32[256,1024]{1,0:T(8,128)S(1)} custom-call(bf16[8,272,128]{2,1,0:T(8,128)(2,1)S(1)} %collective-permute-done.1.refs_0_, bf16[8,272,128]{2,1,0:T(8,128)(2,1)S(1)} %collective-permute-done.refs_0_.refs_1_.part_ref, bf16[1024,128]{1,0:T(8,128)(2,1)S(1)} %get-tuple-element.13.refs_3_.refs_2_.keys_ref, f32[256,1024]{1,0:T(8,128)S(1)} %get-tuple-element.19.refs_3_), custom_call_target="tpu_custom_call" | custom-call | flops 262144 | bytes 16384 | tf_op jit(solution)/shard_map/z_own/pallas_call | solution.py:186
  60.6 0.0 collective-permute-done.4.other_ref
  60.6 2.0 %finish.1 = f32[256,1024]{1,0:T(8,128)} custom-call(bf16[8,272,128]{2,1,0:T(8,128)(2,1)S(1)} %collective-permute-done.refs_0_.refs_1_.part_ref, bf16[1024,128]{1,0:T(8,128)(2,1)S(1)} %get-tuple-element.13.refs_3_.refs_2_.keys_ref, f32[256,1024]{1,0:T(8,128)S(1)} %z_own.1.total_ref, s32[32,256]{1,0:T(8,128)S(1)} %get-tuple-element.20.reach_ref, ...), custom_call_target="tpu_custom_call" | custom-call | flops 131072 | bytes 16384 | tf_op jit(solution)/shard_map/finish/pallas_call | solution.py:226
Async XLA Ops:
  2.5 41.0 %copy-start = (bf16[1024,128]{1,0:T(8,128)(2,1)S(1)}, bf16[1024,128]{1,0:T(8,128)(2,1)}, u32[]{:S(2)}) copy-start(bf16[1024,128]{1,0:T(8,128)(2,1)} %raw_ref.1) | copy-start | bytes 786436
  34.1 15.1 %collective-permute-start.2 = (bf16[8,272,128]{2,1,0:T(8,128)(2,1)S(1)}, bf16[8,272,128]{2,1,0:T(8,128)(2,1)S(1)}, u32[]{:S(2)}, u32[]{:S(2)}) collective-permute-start(bf16[8,272,128]{2,1,0:T(8,128)(2,1)S(1)} %all_to_all.5.part_ref.refs_0_), channel_id=1, source_target_pairs={{0,11},{1,8},{2,9},{3,10},{8,19},{9,16},{10,17},{11,18},{16,27},{1... | collective-permute-start | bytes 1671176 | tf_op jit(solution)/shard_map/ppermute | solution.py:267
  36.1 17.0 %collective-permute-start.1 = (bf16[8,272,128]{2,1,0:T(8,128)(2,1)S(1)}, bf16[8,272,128]{2,1,0:T(8,128)(2,1)S(1)}, u32[]{:S(2)}, u32[]{:S(2)}) collective-permute-start(bf16[8,272,128]{2,1,0:T(8,128)(2,1)S(1)} %all_to_all.5.part_ref.refs_0_), channel_id=1, source_target_pairs={{0,8},{1,9},{2,10},{3,11},{8,16},{9,17},{10,18},{11,19},{16,24},{1... | collective-permute-start | bytes 1671176 | tf_op jit(solution)/shard_map/ppermute | solution.py:268
  39.3 15.2 %collective-permute-start = (bf16[8,272,128]{2,1,0:T(8,128)(2,1)S(1)}, bf16[8,272,128]{2,1,0:T(8,128)(2,1)S(1)}, u32[]{:S(2)}, u32[]{:S(2)}) collective-permute-start(bf16[8,272,128]{2,1,0:T(8,128)(2,1)S(1)} %all_to_all.5.part_ref.refs_0_), channel_id=1, source_target_pairs={{0,1},{1,2},{2,3},{3,0},{8,9},{9,10},{10,11},{11,8},{16,17},{17,18... | collective-permute-start | bytes 1671176 | tf_op jit(solution)/shard_map/ppermute | solution.py:269
  43.5 0.7 %copy-start.1 = (f32[128]{0:T(128)S(1)}, f32[128]{0:T(128)}, u32[]{:S(2)}) copy-start(f32[128]{0:T(128)} %param.12) | copy-start | bytes 1540
  43.5 0.7 %copy-start.2 = (f32[128]{0:T(128)S(1)}, f32[128]{0:T(128)}, u32[]{:S(2)}) copy-start(f32[128]{0:T(128)} %param.13) | copy-start | bytes 1540
  45.8 4.7 %collective-permute-start.3 = (bf16[1024,128]{1,0:T(8,128)(2,1)S(1)}, bf16[1024,128]{1,0:T(8,128)(2,1)S(1)}, u32[]{:S(2)}, u32[]{:S(2)}) collective-permute-start(bf16[1024,128]{1,0:T(8,128)(2,1)S(1)} %get-tuple-element.13.refs_3_.refs_2_.keys_ref), channel_id=1, source_target_pairs={{0,4},{4,0},{1,5},{5,1},{2,6},{6,2},{3,7},{7,3},{8,12},{12,8},{9,1... | collective-permute-start | bytes 786440 | tf_op jit(solution)/shard_map/ppermute | solution.py:273
  55.8 4.8 %collective-permute-start.4 = (bf16[256,1024]{1,0:T(8,128)(2,1)S(1)}, bf16[256,1024]{1,0:T(8,128)(2,1)S(1)}, u32[]{:S(2)}, u32[]{:S(2)}) collective-permute-start(bf16[256,1024]{1,0:T(8,128)(2,1)S(1)} %x_other.1), channel_id=1, source_target_pairs={{0,4},{4,0},{1,5},{5,1},{2,6},{6,2},{3,7},{7,3},{8,12},{12,8},{9,1... | collective-permute-start | bytes 1572872 | tf_op jit(solution)/shard_map/ppermute | solution.py:280
